TPU v7x, 512 devices: a whole 4x4x16 slice. The times are simulated.
512 devices in a mesh: dp: 2 (over y_lo), tm: 8 (over x, core), space: 32 (over y_hi, z).
Axes of the slice: x: 4, y: 4 (y_hi: 2, y_lo: 2; y = y_hi * 2 + y_lo), z: 16, core: 2. Of those that a mesh axis runs over, the one named last changes fastest.
Arguments:
- inputs: bfloat16 [2, 16, 64, 64, 256], P('dp', 'tm', 'space'), may hold values from -6 to 6
- cotangent: bfloat16 [2, 32, 128, 128, 128], P('dp', 'tm', 'space'), may hold values from -6 to 6
- spatial_weight: bfloat16 [3, 3, 256, 256], replicated, may hold values from -0.125 to 0.125
- time_weight: bfloat16 [3, 256, 256], replicated, may hold values from -0.21875 to 0.21875
- up_weight: bfloat16 [256, 1024], replicated, may hold values from -0.375 to 0.375
Outputs:
- input_grad: bfloat16 [2, 16, 64, 64, 256], P('dp', 'tm', 'space')
- spatial_grad: float32 [3, 3, 256, 256], P(None, None, None, 'space')
- time_grad: float32 [3, 256, 256], P(None, None, 'space')
- up_grad: float32 [256, 1024], P(None, 'space')
All inputs are finite; a program needn't handle non-finite values.
Results may differ from a plain program's by a relative error of at most 0.0051.
Values may be sent and summed in bfloat16 or wider, within the bound.
No kernel may reach another device: no remote copies, remote signals or barrier semaphores. Data moves between devices by JAX's collectives and lax.ppermute only.
A program may use at most 64 MiB of HBM per device.

v0:
```python
import jax
import jax.numpy as jnp
from jax import lax
from jax.experimental import pallas as pl
from jax.experimental.pallas import tpu as pltpu
from jax.sharding import Mesh, PartitionSpec as P

epsilon = 1e-06
TIME = ("x", "core")
SPACE = ("y_hi", "z")
GROUP = ("y_lo", "x", "core")
PLANE = ("y_lo", "x", "y_hi")
C = 256
W = 64
FRAMES = 2
ROWS = 2
PIX = FRAMES * ROWS * W
SPACES = 32
MEMBERS = 16
bf16 = jnp.bfloat16
f32 = jnp.float32


def dot(a, b):
    return lax.dot_general(a, b, (((1,), (0,)), ((), ())), preferred_element_type=f32)


def dot_bt(a, b):
    return lax.dot_general(a, b, (((1,), (1,)), ((), ())), preferred_element_type=f32)


def dot_at(a, b):
    return lax.dot_general(a, b, (((0,), (0,)), ((), ())), preferred_element_type=f32)


def column():
    return lax.broadcasted_iota(jnp.int32, (PIX, C), 0) & (W - 1)


def from_left(value):
    return jnp.where(column() == 0, 0.0, pltpu.roll(value, 1, 0))


def from_right(value):
    return jnp.where(column() == W - 1, 0.0, pltpu.roll(value, PIX - 1, 0))


def call(kernel, outs, flops, *operands, **given):
    moved = sum(v.size * v.dtype.itemsize for v in operands)
    moved += sum(s.size * s.dtype.itemsize for s in jax.tree.leaves(outs))
    return pl.pallas_call(
        kernel,
        out_shape=outs,
        compiler_params=pltpu.CompilerParams(vmem_limit_bytes=40 << 20),
        cost_estimate=pl.CostEstimate(flops=flops, bytes_accessed=moved, transcendentals=0),
        **given,
    )(*operands)


def with_scalars(operands):
    specs = [pl.BlockSpec(memory_space=pltpu.SMEM)]
    return specs + [pl.BlockSpec(memory_space=pltpu.VMEM)] * (len(operands) - 1)


def shape(dims, dtype):
    return jax.ShapeDtypeStruct(dims, dtype)


def arranged(cot_ref, up_ref):
    row = lax.broadcasted_iota(jnp.int32, (2 * W, 2 * W), 0)
    col = lax.broadcasted_iota(jnp.int32, (2 * W, 2 * W), 1)
    order = (col == 2 * (row & (W - 1)) + (row >> 6)).astype(f32).astype(bf16)
    for frame in range(FRAMES):
        for height in range(ROWS):
            first = (frame * ROWS + height) * W
            for t in range(2):
                pair = jnp.concatenate(
                    [cot_ref[2 * frame + t, 2 * height + p] for p in range(2)], axis=1
                )
                pair = dot(order, pair).astype(bf16)
                for p in range(2):
                    for q in range(2):
                        up_ref[2 * t + p, first : first + W, q * 128 : q * 128 + 128] = pair[
                            q * W : q * W + W, p * 128 : p * 128 + 128
                        ]


def state_of(up_ref, weight_ref):
    state = None
    for at in range(4):
        part = dot_bt(up_ref[at], weight_ref[:, at * C : at * C + C])
        state = part if state is None else state + part
    return state


def state_kernel(cot_ref, weight_ref, up_ref, state_ref, time_cot_ref):
    arranged(cot_ref, up_ref)
    state = state_of(up_ref, weight_ref)
    state_ref[...] = state
    time_cot_ref[...] = state.astype(bf16)


def later_kernel(cot_ref, weight_ref, up_ref, time_cot_ref):
    arranged(cot_ref, up_ref)
    time_cot_ref[...] = state_of(up_ref, weight_ref).astype(bf16)


def rows_at(block, low, high, offset):
    if offset == 0:
        return block[...].reshape(PIX, C)
    parts = []
    for frame in range(FRAMES):
        if offset < 0:
            parts += [low[frame], block[frame, 0]]
        else:
            parts += [block[frame, 1], high[frame]]
    return jnp.concatenate(parts, axis=0)


def put(core_ref, mine_ref, other_ref, block, start, value):
    first_core = core_ref[0] == 0
    value = value.astype(bf16)
    left, right = value[:, :, :128], value[:, :, 128:]
    count = value.shape[0]
    mine_ref[block, start : start + count] = jnp.where(first_core, left, right)
    other_ref[block, start : start + count] = jnp.where(first_core, right, left)


def paired(one, two):
    return jnp.concatenate([one.reshape(SPACES, 8, C), two.reshape(SPACES, 8, C)], axis=1)


def forward_kernel(
    core_ref, in_ref, low_ref, high_ref, spatial_ref, cot_ref, later_cot_ref, time_ref,
    act_ref, pre_ref, mine_ref, other_ref,
):
    half = ROWS * W
    taps = [None] * 3
    for i in range(3):
        rows = rows_at(in_ref, low_ref, high_ref, i - 1)
        for j in range(3):
            part = dot(rows, spatial_ref[i, j])
            taps[j] = part if taps[j] is None else taps[j] + part
    pre_act = from_left(taps[0]) + taps[1] + from_right(taps[2])
    scale = jnp.sqrt(jnp.mean(pre_act * pre_act, -1, keepdims=True) + epsilon)
    normed = pre_act / scale
    sig = 1.0 / (1.0 + jnp.exp(-normed))
    act_ref[...] = (normed / (1.0 + jnp.exp(-normed))).astype(bf16)
    middle = jnp.concatenate([cot_ref[half:, :], later_cot_ref[:half, :]], axis=0)
    act_grad = dot_bt(cot_ref[...], time_ref[0]) + dot_bt(middle, time_ref[1])
    act_grad = act_grad + dot_bt(later_cot_ref[...], time_ref[2])
    norm_grad = act_grad * sig * (1.0 + normed * (1.0 - sig))
    mean = jnp.mean(norm_grad * normed, -1, keepdims=True)
    pre = ((norm_grad - normed * mean) / scale).astype(bf16)
    pre_ref[...] = pre
    wide = pre.astype(f32)
    shifted = [from_right(wide).astype(bf16), pre, from_left(wide).astype(bf16)]

    def tap(at):
        return dot_at(shifted[at % 3], rows_at(in_ref, low_ref, high_ref, at // 3 - 1))

    for block in range(4):
        value = paired(tap(2 * block), tap(2 * block + 1))
        put(core_ref, mine_ref, other_ref, block, 0, value)


def rest_kernel(
    core_ref, in_ref, high_ref, pre_ref, act_ref, cot_ref, later_cot_ref, up_ref, later_up_ref,
    time_ref, mine_ref, other_ref,
):
    half = ROWS * W
    act = act_ref[...]
    middle = jnp.concatenate([cot_ref[half:, :], later_cot_ref[:half, :]], axis=0)
    last = from_left(pre_ref[...].astype(f32)).astype(bf16)
    value = paired(dot_at(last, rows_at(in_ref, None, high_ref, 1)), dot_at(cot_ref[...], act))
    put(core_ref, mine_ref, other_ref, 0, 0, value)
    value = paired(dot_at(middle, act), dot_at(later_cot_ref[...], act))
    put(core_ref, mine_ref, other_ref, 1, 0, value)
    own = in_ref[...].reshape(PIX, C)
    mixed = [
        (own.astype(f32) + dot(act, time_ref[0])).astype(bf16),
        dot(act, time_ref[1]).astype(bf16),
        dot(act, time_ref[2]).astype(bf16),
    ]
    for at in range(4):
        part = dot_at(up_ref[at], mixed[0])
        part = part + dot_at(up_ref[at, half:, :], mixed[1][:half, :])
        part = part + dot_at(later_up_ref[at, :half, :], mixed[1][half:, :])
        part = part + dot_at(later_up_ref[at], mixed[2])
        part = part.reshape(8, 32, C)
        for low in range(2):
            rows = part[:, low * 16 : low * 16 + 16]
            put(core_ref, mine_ref, other_ref, 2 + low, at * 8, rows)


def swap_sum_kernel(mine_one, mine_two, arrived_one, arrived_two, out_ref, held_ref, sems):
    copies = []
    for at in range(8):
        mine = mine_one if at < 4 else mine_two
        arrived = arrived_one if at < 4 else arrived_two
        total = mine[at % 4].astype(f32) + arrived[at % 4].astype(f32)
        held_ref[at] = total.astype(bf16)
        copies.append(pltpu.make_async_copy(held_ref.at[at], out_ref.at[at], sems.at[at]))
        copies[-1].start()
    for copy in copies:
        copy.wait()


def plane_sum_kernel(parts_ref, out_ref):
    total = parts_ref[0].astype(f32)
    for at in range(1, 16):
        total = total + parts_ref[at].astype(f32)
    out_ref[...] = total.astype(bf16)


def depth_sum_kernel(parts_ref, out_ref):
    total = parts_ref[0].astype(f32)
    for at in range(1, 16):
        total = total + parts_ref[at].astype(f32)
    for at in range(MEMBERS):
        out_ref[at] = total


def input_grad_kernel(state_ref, pre_ref, low_ref, high_ref, weight_ref, out_ref):
    taps = [None] * 3
    for i in range(3):
        rows = rows_at(pre_ref, low_ref, high_ref, 1 - i)
        for j in range(3):
            part = dot_bt(rows, weight_ref[i, j])
            taps[j] = part if taps[j] is None else taps[j] + part
    total = state_ref[...] + (from_right(taps[0]) + taps[1] + from_left(taps[2]))
    out_ref[...] = total.astype(bf16)


def unpack_kernel(in_ref, spatial_ref, time_ref, up_ref):
    for block in range(6):
        for lane in range(2):
            for low in range(2):
                at = 2 * block + low
                value = in_ref[2 * block + lane, low * 8 : low * 8 + 8, :]
                if at < 9:
                    spatial_ref[at, :, lane * 128 : lane * 128 + 128] = value
                else:
                    time_ref[at - 9, :, lane * 128 : lane * 128 + 128] = value
    for low in range(2):
        for lane in range(2):
            up_ref[low * 16 : low * 16 + 16, lane * 128 : lane * 128 + 128] = in_ref[
                12 + 2 * low + lane
            ]


def states(cotangent, up_weight):
    outs = (shape((4, PIX, C), bf16), shape((PIX, C), f32), shape((PIX, C), bf16))
    return call(state_kernel, outs, 10 * PIX * C * C, cotangent, up_weight)


def later_states(cotangent, up_weight):
    outs = (shape((4, PIX, C), bf16), shape((PIX, C), bf16))
    return call(later_kernel, outs, 10 * PIX * C * C, cotangent, up_weight)


def forward(*operands):
    flat, half = shape((PIX, C), bf16), shape((4, SPACES, 16, 128), bf16)
    specs = with_scalars(operands)
    outs = (flat, flat, half, half)
    return call(forward_kernel, outs, 40 * PIX * C * C, *operands, in_specs=specs)


def rest(*operands):
    half = shape((4, SPACES, 16, 128), bf16)
    specs = with_scalars(operands)
    return call(rest_kernel, (half, half), 38 * PIX * C * C, *operands, in_specs=specs)


def swap_sum(*operands):
    out = shape((8, SPACES, 16, 128), bf16)
    return call(
        swap_sum_kernel,
        out,
        0,
        *operands,
        out_specs=pl.BlockSpec(memory_space=pl.ANY),
        scratch_shapes=[pltpu.VMEM(out.shape, bf16), pltpu.SemaphoreType.DMA((8,))],
    )


def input_gradient(*operands):
    outs = (shape((PIX, C), bf16),)
    return call(input_grad_kernel, outs, 18 * PIX * C * C, *operands)[0]


def unpacked(gathered):
    outs = (shape((9, 8, C), f32), shape((3, 8, C), f32), shape((32, C), f32))
    return call(unpack_kernel, outs, 0, gathered)


def halo(block, after):
    even = (lax.axis_index(SPACE) & 1) == 0
    top, bottom = block[:, 0], block[:, ROWS - 1]
    pairs = [[(i, i + 1) for i in range(start, SPACES - 1, 2)] for start in (0, 1)]
    pairs = [found + [(b, a) for a, b in found] for found in pairs]
    first = lax.ppermute(jnp.where(even, bottom, top), SPACE, pairs[0])
    second = lax.ppermute(jnp.where(even, top, bottom), SPACE, pairs[1])
    first, second, after = lax.optimization_barrier((first, second, after))
    return jnp.where(even, second, first), jnp.where(even, first, second), after


def local(inputs, cotangent, spatial_weight, time_weight, up_weight):
    tile = inputs.reshape(FRAMES, ROWS, W, C)
    cotangent = cotangent.reshape(2 * FRAMES, 2 * ROWS, 2 * W, -1)
    later = lax.ppermute(cotangent, TIME, [(i + 1, i) for i in range(7)])
    upward, state_grad, time_cot = states(cotangent, up_weight)
    later, time_cot = lax.optimization_barrier((later, time_cot))
    later_up, later_cot = later_states(later, up_weight)
    low, high, later_cot = halo(tile, later_cot)
    core = lax.axis_index("core").astype(jnp.int32).reshape(1)
    activated, pre_grad, mine_one, other_one = forward(
        core, tile, low, high, spatial_weight, time_cot, later_cot, time_weight
    )
    other_one = lax.ppermute(other_one, "core", [(0, 1), (1, 0)])
    mine_two, other_two = rest(
        core, tile, high, pre_grad, activated, time_cot, later_cot, upward, later_up, time_weight
    )
    other_one, other_two = lax.optimization_barrier((other_one, other_two))
    other_two = lax.ppermute(other_two, "core", [(0, 1), (1, 0)])
    value = swap_sum(mine_one, mine_two, other_one, other_two)
    pre_tile = pre_grad.reshape(FRAMES, ROWS, W, C)
    held, value = lax.optimization_barrier((pre_tile, value))
    value = lax.all_to_all(value.reshape(16, 16, 16, 128), PLANE, 0, 0)
    pre_low, pre_high, state_grad = halo(held, state_grad)
    input_grad = input_gradient(state_grad, pre_tile, pre_low, pre_high, spatial_weight)
    value, input_grad = lax.optimization_barrier((value, input_grad))
    value = call(plane_sum_kernel, (shape((16, 16, 128), bf16),), 0, value)[0]
    value = lax.all_to_all(value, "z", 0, 0)
    value = call(depth_sum_kernel, (shape((MEMBERS, 16, 128), f32),), 0, value)[0]
    spatial_grad, time_grad, up_grad = unpacked(lax.all_to_all(value, GROUP, 0, 0))
    return (
        input_grad.reshape(inputs.shape),
        jnp.swapaxes(spatial_grad.reshape(3, 3, 8, C), 2, 3),
        jnp.swapaxes(time_grad, 1, 2),
        jnp.swapaxes(up_grad, 0, 1),
    )


def solution(mesh):
    whole = Mesh(mesh.devices.reshape(2, 4, 2, 2, 16), ("y_lo", "x", "core", "y_hi", "z"))
    tile = P("y_lo", TIME, SPACE, None, None)
    return jax.shard_map(
        local,
        mesh=whole,
        in_specs=(tile, tile, P(), P(), P()),
        out_specs=(tile, P(None, None, None, SPACE), P(None, None, SPACE), P(None, SPACE)),
        check_vma=False,
    )
```

profile of v0, /device:TPU:1, one launch (start us, length us, event | category | flops | bytes accessed | tf_op | source)
XLA Modules:
  0.0 88.8 jit_solution(5746455336369267829)
XLA Ops:
  0.6 0.0 copy-start.1
  0.6 8.9 %collective-permute-start.2 = (bf16[4,4,128,128]{3,2,1,0:T(8,128)(2,1)}, bf16[4,4,128,128]{3,2,1,0:T(8,128)(2,1)S(1)}, u32[]{:S(2)}, u32[]{:S(2)}) collective-permute-start(bf16[4,4,128,128]{3,2,1,0:T(8,128)(2,1)} %bitcast.24), channel_id=1, source_target_pairs={{32,0},{64,32},{96,64},{128,96},{160,128},{192,160},{224,192},{33,... | collective-permute-start | bytes 1572872 | tf_op jit(solution)/shard_map/ppermute | solution.py:311
  9.6 0.9 %copy.22 = bf16[1,2,2,64,256]{4,3,1,2,0:T(8,128)(2,1)S(1)} copy(bf16[1,2,2,64,256]{4,3,2,1,0:T(8,128)(2,1)} %param.5) | data formatting | bytes 262144 | tf_op args[0]
  10.5 0.7 collective-permute-start.1
  11.2 1.9 %collective-permute-start = (bf16[2,64,256]{2,1,0:T(8,128)(2,1)S(1)}, bf16[2,64,256]{2,1,0:T(8,128)(2,1)S(1)}, u32[]{:S(2)}, u32[]{:S(2)}) collective-permute-start(bf16[2,64,256]{2,1,0:T(8,128)(2,1)S(1)} %get-tuple-element.67), channel_id=1, source_target_pairs={{0,1},{2,3},{4,5},{6,7},{8,9},{10,11},{12,13},{14,15},{16,17},{18,... | collective-permute-start | bytes 196616 | tf_op jit(solution)/shard_map/ppermute | solution.py:302
  13.1 0.0 copy-start
  13.1 1.0 %copy-done = bf16[256,1024]{1,0:T(8,128)(2,1)S(1)} copy-done((bf16[256,1024]{1,0:T(8,128)(2,1)S(1)}, bf16[256,1024]{1,0:T(8,128)(2,1)}, u32[]{:S(2)}) %copy-start) | copy-done | bytes 524312
  14.2 0.0 copy-start.3
  14.2 1.0 %copy-done.3 = bf16[1,4,4,128,128]{4,3,2,1,0:T(8,128)(2,1)S(1)} copy-done((bf16[1,4,4,128,128]{4,3,2,1,0:T(8,128)(2,1)S(1)}, bf16[1,4,4,128,128]{4,3,2,1,0:T(8,128)(2,1)}, u32[]{:S(2)}) %copy-start.3) | copy-done | bytes 524312
  15.2 0.0 copy-start.2
  15.2 0.0 copy-start.4
  15.2 0.0 copy-start.5
  15.2 0.5 shard_map.84
  15.8 0.0 collective-permute-done.2.cot_ref
  15.8 0.0 copy-done.1
  15.8 0.5 shard_map.85
  16.3 0.0 collective-permute-done.1
  16.3 0.6 collective-permute-done
  16.9 0.0 copy-done.2
  16.9 0.0 copy-done.4
  16.9 0.0 copy-done.5
  16.9 1.3 %shard_map.86 = (bf16[256,256]{1,0:T(8,128)(2,1)S(1)}, bf16[256,256]{1,0:T(8,128)(2,1)S(1)}, bf16[4,32,16,128]{3,2,1,0:T(8,128)(2,1)S(1)}, bf16[4,32,16,128]{3,2,1,0:T(8,128)(2,1)S(1)}) custom-call(s32[1]{0:T(128)} %bitcast.core_ref, bf16[2,2,64,256]{3,2,1,0:T(8,128)(2,1)S(1)} %bitcast.26, bf16[2,64,256]{2,1,0:T(8,128)(2,1)S(1)} %get-tuple-element.65.low_ref, ...), custom_call_target="tpu_custom_call" | custom-call | flops 671088640 | bytes 3407876 | tf_op jit(solution)/shard_map/pallas_call | solution.py:51
  18.3 2.3 %collective-permute-start.3 = (bf16[4,32,16,128]{3,2,1,0:T(8,128)(2,1)S(1)}, bf16[4,32,16,128]{3,2,1,0:T(8,128)(2,1)S(1)}, u32[]{:S(2)}, u32[]{:S(2)}) collective-permute-start(bf16[4,32,16,128]{3,2,1,0:T(8,128)(2,1)S(1)} %get-tuple-element.45), channel_id=1, source_target_pairs={{0,32},{32,0},{1,33},{33,1},{2,34},{34,2},{3,35},{35,3},{4,36},{36... | collective-permute-start | bytes 1572872 | tf_op jit(solution)/shard_map/ppermute | solution.py:320
  20.6 1.1 %shard_map.87 = (bf16[4,32,16,128]{3,2,1,0:T(8,128)(2,1)S(1)}, bf16[4,32,16,128]{3,2,1,0:T(8,128)(2,1)S(1)}) custom-call(s32[1]{0:T(128)} %bitcast.core_ref, bf16[2,2,64,256]{3,2,1,0:T(8,128)(2,1)S(1)} %bitcast.27, bf16[2,64,256]{2,1,0:T(8,128)(2,1)S(1)} %get-tuple-element.64.high_ref, bf16[256,256]{1,0:T(8,128)(2,1)S(1)} %get-tuple-element.39.pre_ref, ...), custom_call_target="tpu_custom_call" | custom-call | flops 637534208 | bytes 3211268 | tf_op jit(solution)/shard_map/pallas_call | solution.py:51
  21.7 0.4 collective-permute-done.3.arrived_one
  22.1 2.3 %collective-permute-start.4 = (bf16[4,32,16,128]{3,2,1,0:T(8,128)(2,1)S(1)}, bf16[4,32,16,128]{3,2,1,0:T(8,128)(2,1)S(1)}, u32[]{:S(2)}, u32[]{:S(2)}) collective-permute-start(bf16[4,32,16,128]{3,2,1,0:T(8,128)(2,1)S(1)} %get-tuple-element.48), channel_id=1, source_target_pairs={{0,32},{32,0},{1,33},{33,1},{2,34},{34,2},{3,35},{35,3},{4,36},{36... | collective-permute-start | bytes 1572872 | tf_op jit(solution)/shard_map/ppermute | solution.py:325
  24.4 1.5 %collective-permute-done.4.arrived_two = bf16[4,32,16,128]{3,2,1,0:T(8,128)(2,1)S(1)} collective-permute-done((bf16[4,32,16,128]{3,2,1,0:T(8,128)(2,1)S(1)}, bf16[4,32,16,128]{3,2,1,0:T(8,128)(2,1)S(1)}, u32[]{:S(2)}, u32[]{:S(2)}) %collective-permute-start.4) | collective-permute-done | bytes 524320 | tf_op jit(solution)/shard_map/ppermute | solution.py:325
  25.9 1.1 %shard_map.88 = bf16[8,32,16,128]{3,2,1,0:T(8,128)(2,1)} custom-call(bf16[4,32,16,128]{3,2,1,0:T(8,128)(2,1)S(1)} %get-tuple-element.40.mine_one, bf16[4,32,16,128]{3,2,1,0:T(8,128)(2,1)S(1)} %get-tuple-element.44.mine_two, bf16[4,32,16,128]{3,2,1,0:T(8,128)(2,1)S(1)} %collective-permute-done.3.arrived_one, ...), custom_call_target="tpu_custom_call" | custom-call | bytes 3145728 | tf_op jit(solution)/shard_map/pallas_call | solution.py:51
  27.0 12.7 %all-to-all-start = ((bf16[16,16,16,128]{3,2,1,0:T(8,128)(2,1)}), bf16[16,16,16,128]{3,2,1,0:T(8,128)(2,1)S(1)}, u32[]{:S(2)}, u32[]{:S(2)}) async-start(bf16[16,16,16,128]{3,2,1,0:T(8,128)(2,1)} %bitcast.7), calls=%async_computation | async-start | bytes 2097152 | tf_op jit(solution)/shard_map/all_to_all | solution.py:329
  39.8 0.7 collective-permute-start.6
  40.4 4.1 %collective-permute-start.5 = (bf16[2,64,256]{2,1,0:T(8,128)(2,1)S(1)}, bf16[2,64,256]{2,1,0:T(8,128)(2,1)S(1)}, u32[]{:S(2)}, u32[]{:S(2)}) collective-permute-start(bf16[2,64,256]{2,1,0:T(8,128)(2,1)S(1)} %get-tuple-element.63), channel_id=1, source_target_pairs={{0,1},{2,3},{4,5},{6,7},{8,9},{10,11},{12,13},{14,15},{16,17},{18,... | collective-permute-start | bytes 196616 | tf_op jit(solution)/shard_map/ppermute | solution.py:302
  44.5 0.0 collective-permute-done.6
  44.5 1.9 %collective-permute-done.5 = bf16[2,64,256]{2,1,0:T(8,128)(2,1)S(1)} collective-permute-done((bf16[2,64,256]{2,1,0:T(8,128)(2,1)S(1)}, bf16[2,64,256]{2,1,0:T(8,128)(2,1)S(1)}, u32[]{:S(2)}, u32[]{:S(2)}) %collective-permute-start.5) | collective-permute-done | bytes 65568 | tf_op jit(solution)/shard_map/ppermute | solution.py:302
  46.5 1.2 %shard_map.89 = bf16[256,256]{1,0:T(8,128)(2,1)} custom-call(f32[256,256]{1,0:T(8,128)S(1)} %get-tuple-element.52.state_ref, bf16[2,2,64,256]{3,2,1,0:T(8,128)(2,1)S(1)} %bitcast.23, bf16[2,64,256]{2,1,0:T(8,128)(2,1)S(1)} %get-tuple-element.61.low_ref, bf16[2,64,256]{2,1,0:T(8,128)(2,1)S(1)} %get-tuple-element.60.high_ref, ...), custom_call_target="tpu_custom_call" | custom-call | flops 301989888 | bytes 1835008 | tf_op jit(solution)/shard_map/pallas_call | solution.py:51
  47.7 10.6 %all-to-all-done.parts_ref = bf16[16,16,16,128]{3,2,1,0:T(8,128)(2,1)S(1)} async-done(((bf16[16,16,16,128]{3,2,1,0:T(8,128)(2,1)}), bf16[16,16,16,128]{3,2,1,0:T(8,128)(2,1)S(1)}, u32[]{:S(2)}, u32[]{:S(2)}) %all-to-all-start) | async-done | bytes 1048608 | tf_op jit(solution)/shard_map/all_to_all | solution.py:329
  58.3 0.1 shard_map.90
  58.4 15.7 %all_to_all.15.parts_ref = bf16[16,16,128]{2,1,0:T(8,128)(2,1)S(1)} all-to-all(bf16[16,16,128]{2,1,0:T(8,128)(2,1)S(1)} %shard_map.90), channel_id=1, replica_groups=mesh['y_lo'=2,'x'=4,'core'=2,'y_hi'=2,'z'=16] {'z'}, dimensions={0} | all-to-all | bytes 131072 | tf_op jit(solution)/shard_map/all_to_all | solution.py:334
  74.1 14.0 %all_to_all.16.in_ref = f32[16,16,128]{2,1,0:T(8,128)S(1)} all-to-all(f32[16,16,128]{2,1,0:T(8,128)S(1)} %shard_map.91), channel_id=1, replica_groups=mesh['y_lo'=2,'x'=4,'core'=2,'y_hi'=2,'z'=16] {'y_lo','x','core'}, dimensions={0} | all-to-all | bytes 262144 | tf_op jit(solution)/shard_map/all_to_all | solution.py:336
  88.1 0.7 shard_map.92
  (5 shorter events, 0.1 us)
Async XLA Ops:
  0.6 15.1 %copy-start.1 = (bf16[256,1024]{1,0:T(8,128)(2,1)S(1)}, bf16[256,1024]{1,0:T(8,128)(2,1)}, u32[]{:S(2)}) copy-start(bf16[256,1024]{1,0:T(8,128)(2,1)} %weight_ref.4) | copy-start | bytes 1572868
  0.6 15.1 %collective-permute-start.2 = (bf16[4,4,128,128]{3,2,1,0:T(8,128)(2,1)}, bf16[4,4,128,128]{3,2,1,0:T(8,128)(2,1)S(1)}, u32[]{:S(2)}, u32[]{:S(2)}) collective-permute-start(bf16[4,4,128,128]{3,2,1,0:T(8,128)(2,1)} %bitcast.24), channel_id=1, source_target_pairs={{32,0},{64,32},{96,64},{128,96},{160,128},{192,160},{224,192},{33,... | collective-permute-start | bytes 1572872 | tf_op jit(solution)/shard_map/ppermute | solution.py:311
  10.5 5.8 %collective-permute-start.1 = (bf16[2,64,256]{2,1,0:T(8,128)(2,1)S(1)}, bf16[2,64,256]{2,1,0:T(8,128)(2,1)S(1)}, u32[]{:S(2)}, u32[]{:S(2)}) collective-permute-start(bf16[2,64,256]{2,1,0:T(8,128)(2,1)S(1)} %get-tuple-element.66), channel_id=1, source_target_pairs={{1,2},{3,4},{5,6},{7,8},{9,10},{11,12},{13,14},{15,16},{17,18},{19... | collective-permute-start | bytes 196616 | tf_op jit(solution)/shard_map/ppermute | solution.py:303
  11.2 5.7 %collective-permute-start = (bf16[2,64,256]{2,1,0:T(8,128)(2,1)S(1)}, bf16[2,64,256]{2,1,0:T(8,128)(2,1)S(1)}, u32[]{:S(2)}, u32[]{:S(2)}) collective-permute-start(bf16[2,64,256]{2,1,0:T(8,128)(2,1)S(1)} %get-tuple-element.67), channel_id=1, source_target_pairs={{0,1},{2,3},{4,5},{6,7},{8,9},{10,11},{12,13},{14,15},{16,17},{18,... | collective-permute-start | bytes 196616 | tf_op jit(solution)/shard_map/ppermute | solution.py:302
  13.1 1.0 %copy-start = (bf16[256,1024]{1,0:T(8,128)(2,1)S(1)}, bf16[256,1024]{1,0:T(8,128)(2,1)}, u32[]{:S(2)}) copy-start(bf16[256,1024]{1,0:T(8,128)(2,1)} %weight_ref.4) | copy-start | bytes 1572868
  14.2 1.0 %copy-start.3 = (bf16[1,4,4,128,128]{4,3,2,1,0:T(8,128)(2,1)S(1)}, bf16[1,4,4,128,128]{4,3,2,1,0:T(8,128)(2,1)}, u32[]{:S(2)}) copy-start(bf16[1,4,4,128,128]{4,3,2,1,0:T(8,128)(2,1)} %param.6) | copy-start | bytes 1572868
  15.2 1.7 %copy-start.2 = (bf16[3,3,256,256]{3,2,1,0:T(8,128)(2,1)S(1)}, bf16[3,3,256,256]{3,2,1,0:T(8,128)(2,1)}, u32[]{:S(2)}) copy-start(bf16[3,3,256,256]{3,2,1,0:T(8,128)(2,1)} %weight_ref.5) | copy-start | bytes 3538948
  15.2 1.7 %copy-start.4 = (bf16[1,2,2,64,256]{4,3,2,1,0:T(8,128)(2,1)S(1)}, bf16[1,2,2,64,256]{4,3,2,1,0:T(8,128)(2,1)}, u32[]{:S(2)}) copy-start(bf16[1,2,2,64,256]{4,3,2,1,0:T(8,128)(2,1)} %param.5) | copy-start | bytes 393220
  15.2 1.7 %copy-start.5 = (bf16[3,256,256]{2,1,0:T(8,128)(2,1)S(1)}, bf16[3,256,256]{2,1,0:T(8,128)(2,1)}, u32[]{:S(2)}) copy-start(bf16[3,256,256]{2,1,0:T(8,128)(2,1)} %time_ref.3) | copy-start | bytes 1179652
  18.3 3.8 %collective-permute-start.3 = (bf16[4,32,16,128]{3,2,1,0:T(8,128)(2,1)S(1)}, bf16[4,32,16,128]{3,2,1,0:T(8,128)(2,1)S(1)}, u32[]{:S(2)}, u32[]{:S(2)}) collective-permute-start(bf16[4,32,16,128]{3,2,1,0:T(8,128)(2,1)S(1)} %get-tuple-element.45), channel_id=1, source_target_pairs={{0,32},{32,0},{1,33},{33,1},{2,34},{34,2},{3,35},{35,3},{4,36},{36... | collective-permute-start | bytes 1572872 | tf_op jit(solution)/shard_map/ppermute | solution.py:320
  22.1 3.8 %collective-permute-start.4 = (bf16[4,32,16,128]{3,2,1,0:T(8,128)(2,1)S(1)}, bf16[4,32,16,128]{3,2,1,0:T(8,128)(2,1)S(1)}, u32[]{:S(2)}, u32[]{:S(2)}) collective-permute-start(bf16[4,32,16,128]{3,2,1,0:T(8,128)(2,1)S(1)} %get-tuple-element.48), channel_id=1, source_target_pairs={{0,32},{32,0},{1,33},{33,1},{2,34},{34,2},{3,35},{35,3},{4,36},{36... | collective-permute-start | bytes 1572872 | tf_op jit(solution)/shard_map/ppermute | solution.py:325
  27.0 31.3 %all-to-all-start = ((bf16[16,16,16,128]{3,2,1,0:T(8,128)(2,1)}), bf16[16,16,16,128]{3,2,1,0:T(8,128)(2,1)S(1)}, u32[]{:S(2)}, u32[]{:S(2)}) async-start(bf16[16,16,16,128]{3,2,1,0:T(8,128)(2,1)} %bitcast.7), calls=%async_computation | async-start | bytes 2097152 | tf_op jit(solution)/shard_map/all_to_all | solution.py:329
  39.8 4.8 %collective-permute-start.6 = (bf16[2,64,256]{2,1,0:T(8,128)(2,1)S(1)}, bf16[2,64,256]{2,1,0:T(8,128)(2,1)S(1)}, u32[]{:S(2)}, u32[]{:S(2)}) collective-permute-start(bf16[2,64,256]{2,1,0:T(8,128)(2,1)S(1)} %get-tuple-element.62), channel_id=1, source_target_pairs={{1,2},{3,4},{5,6},{7,8},{9,10},{11,12},{13,14},{15,16},{17,18},{19... | collective-permute-start | bytes 196616 | tf_op jit(solution)/shard_map/ppermute | solution.py:303
  40.4 6.0 %collective-permute-start.5 = (bf16[2,64,256]{2,1,0:T(8,128)(2,1)S(1)}, bf16[2,64,256]{2,1,0:T(8,128)(2,1)S(1)}, u32[]{:S(2)}, u32[]{:S(2)}) collective-permute-start(bf16[2,64,256]{2,1,0:T(8,128)(2,1)S(1)} %get-tuple-element.63), channel_id=1, source_target_pairs={{0,1},{2,3},{4,5},{6,7},{8,9},{10,11},{12,13},{14,15},{16,17},{18,... | collective-permute-start | bytes 196616 | tf_op jit(solution)/shard_map/ppermute | solution.py:302
where the time goes:
time: 89.4 us; the launch traced here: 88.8 us
  starting transfers between devices  33.6 us (38%)
  blocking collectives  29.7 us (33%)
  waiting for transfers between devices  15.1 us (17%)
  Pallas kernels  6.56 us (7%)
  local copies, waits for them, and re-layouts  3.01 us (3%)
    all_to_all x1, blocking collectives, local(): value = lax.all_to_all(value, 'z', 0, 0)  15.7 us
    all_to_all x1, blocking collectives, local(): lax.all_to_all(value, GROUP, 0, 0)  14 us
    all_to_all x1, starting transfers between devices, local(): value = lax.all_to_all(value.reshape(16, 16, 16, 128), PLANE, 0, 0)  12.7 us
    all_to_all x1, waiting for transfers between devices, local(): value = lax.all_to_all(value.reshape(16, 16, 16, 128), PLANE, 0, 0)  10.6 us
    ppermute x1, starting transfers between devices, local(): later = lax.ppermute(cotangent, TIME, [(i + 1, i) for i in range(7)])  8.92 us
    pallas_call x9, Pallas kernels, call(): pl.pallas_call(kernel, out_shape=outs, compiler_params=pltpu.CompilerPara...  6.56 us
    ppermute x2, starting transfers between devices, halo(): first = lax.ppermute(jnp.where(even, bottom, top), SPACE, pairs[0])  6.02 us
    unnamed x13, local copies, waits for them, and re-layouts  3.01 us
  transfers between devices with their start and end apart: 8, of which 5 were waited for; matrix products, arithmetic and copies ran while one was open for 1% of the time, Pallas kernels for 4%

commit v1 on v0

--- a/solution.py
+++ b/solution.py
@@ -93,16 +93,18 @@
     return state
 
 
-def state_kernel(cot_ref, weight_ref, up_ref, state_ref, time_cot_ref):
+def own_kernel(cot_ref, up_ref):
     arranged(cot_ref, up_ref)
+
+
+def state_kernel(
+    cot_ref, up_ref, weight_ref, later_up_ref, state_ref, time_cot_ref, later_cot_ref
+):
     state = state_of(up_ref, weight_ref)
     state_ref[...] = state
     time_cot_ref[...] = state.astype(bf16)
-
-
-def later_kernel(cot_ref, weight_ref, up_ref, time_cot_ref):
-    arranged(cot_ref, up_ref)
-    time_cot_ref[...] = state_of(up_ref, weight_ref).astype(bf16)
+    arranged(cot_ref, later_up_ref)
+    later_cot_ref[...] = state_of(later_up_ref, weight_ref).astype(bf16)
 
 
 def rows_at(block, low, high, offset):
@@ -130,9 +132,9 @@
     return jnp.concatenate([one.reshape(SPACES, 8, C), two.reshape(SPACES, 8, C)], axis=1)
 
 
-def forward_kernel(
-    core_ref, in_ref, low_ref, high_ref, spatial_ref, cot_ref, later_cot_ref, time_ref,
-    act_ref, pre_ref, mine_ref, other_ref,
+def gradients_kernel(
+    core_ref, in_ref, low_ref, high_ref, spatial_ref, cot_ref, later_cot_ref, up_ref, later_up_ref,
+    time_ref, pre_ref, mine_ref, other_ref,
 ):
     half = ROWS * W
     taps = [None] * 3
@@ -145,7 +147,7 @@
     scale = jnp.sqrt(jnp.mean(pre_act * pre_act, -1, keepdims=True) + epsilon)
     normed = pre_act / scale
     sig = 1.0 / (1.0 + jnp.exp(-normed))
-    act_ref[...] = (normed / (1.0 + jnp.exp(-normed))).astype(bf16)
+    act = (normed / (1.0 + jnp.exp(-normed))).astype(bf16)
     middle = jnp.concatenate([cot_ref[half:, :], later_cot_ref[:half, :]], axis=0)
     act_grad = dot_bt(cot_ref[...], time_ref[0]) + dot_bt(middle, time_ref[1])
     act_grad = act_grad + dot_bt(later_cot_ref[...], time_ref[2])
@@ -156,26 +158,16 @@
     wide = pre.astype(f32)
     shifted = [from_right(wide).astype(bf16), pre, from_left(wide).astype(bf16)]
 
+    cots = [cot_ref[...], middle, later_cot_ref[...]]
+
     def tap(at):
-        return dot_at(shifted[at % 3], rows_at(in_ref, low_ref, high_ref, at // 3 - 1))
-
-    for block in range(4):
+        if at < 9:
+            return dot_at(shifted[at % 3], rows_at(in_ref, low_ref, high_ref, at // 3 - 1))
+        return dot_at(cots[at - 9], act)
+
+    for block in range(6):
         value = paired(tap(2 * block), tap(2 * block + 1))
         put(core_ref, mine_ref, other_ref, block, 0, value)
-
-
-def rest_kernel(
-    core_ref, in_ref, high_ref, pre_ref, act_ref, cot_ref, later_cot_ref, up_ref, later_up_ref,
-    time_ref, mine_ref, other_ref,
-):
-    half = ROWS * W
-    act = act_ref[...]
-    middle = jnp.concatenate([cot_ref[half:, :], later_cot_ref[:half, :]], axis=0)
-    last = from_left(pre_ref[...].astype(f32)).astype(bf16)
-    value = paired(dot_at(last, rows_at(in_ref, None, high_ref, 1)), dot_at(cot_ref[...], act))
-    put(core_ref, mine_ref, other_ref, 0, 0, value)
-    value = paired(dot_at(middle, act), dot_at(later_cot_ref[...], act))
-    put(core_ref, mine_ref, other_ref, 1, 0, value)
     own = in_ref[...].reshape(PIX, C)
     mixed = [
         (own.astype(f32) + dot(act, time_ref[0])).astype(bf16),
@@ -190,15 +182,13 @@
         part = part.reshape(8, 32, C)
         for low in range(2):
             rows = part[:, low * 16 : low * 16 + 16]
-            put(core_ref, mine_ref, other_ref, 2 + low, at * 8, rows)
-
-
-def swap_sum_kernel(mine_one, mine_two, arrived_one, arrived_two, out_ref, held_ref, sems):
+            put(core_ref, mine_ref, other_ref, 6 + low, at * 8, rows)
+
+
+def swap_sum_kernel(mine_ref, arrived_ref, out_ref, held_ref, sems):
     copies = []
     for at in range(8):
-        mine = mine_one if at < 4 else mine_two
-        arrived = arrived_one if at < 4 else arrived_two
-        total = mine[at % 4].astype(f32) + arrived[at % 4].astype(f32)
+        total = mine_ref[at].astype(f32) + arrived_ref[at].astype(f32)
         held_ref[at] = total.astype(bf16)
         copies.append(pltpu.make_async_copy(held_ref.at[at], out_ref.at[at], sems.at[at]))
         copies[-1].start()
@@ -249,27 +239,21 @@
             ]
 
 
-def states(cotangent, up_weight):
-    outs = (shape((4, PIX, C), bf16), shape((PIX, C), f32), shape((PIX, C), bf16))
-    return call(state_kernel, outs, 10 * PIX * C * C, cotangent, up_weight)
-
-
-def later_states(cotangent, up_weight):
-    outs = (shape((4, PIX, C), bf16), shape((PIX, C), bf16))
-    return call(later_kernel, outs, 10 * PIX * C * C, cotangent, up_weight)
-
-
-def forward(*operands):
-    flat, half = shape((PIX, C), bf16), shape((4, SPACES, 16, 128), bf16)
+def own_upward(cotangent):
+    return call(own_kernel, (shape((4, PIX, C), bf16),), 2 * PIX * C * C, cotangent)[0]
+
+
+def states(later, upward, up_weight):
+    flat = shape((PIX, C), bf16)
+    outs = (shape((4, PIX, C), bf16), shape((PIX, C), f32), flat, flat)
+    return call(state_kernel, outs, 18 * PIX * C * C, later, upward, up_weight)
+
+
+def gradients(*operands):
+    half = shape((8, SPACES, 16, 128), bf16)
     specs = with_scalars(operands)
-    outs = (flat, flat, half, half)
-    return call(forward_kernel, outs, 40 * PIX * C * C, *operands, in_specs=specs)
-
-
-def rest(*operands):
-    half = shape((4, SPACES, 16, 128), bf16)
-    specs = with_scalars(operands)
-    return call(rest_kernel, (half, half), 38 * PIX * C * C, *operands, in_specs=specs)
+    outs = (shape((PIX, C), bf16), half, half)
+    return call(gradients_kernel, outs, 76 * PIX * C * C, *operands, in_specs=specs)
 
 
 def swap_sum(*operands):
@@ -309,21 +293,16 @@
     tile = inputs.reshape(FRAMES, ROWS, W, C)
     cotangent = cotangent.reshape(2 * FRAMES, 2 * ROWS, 2 * W, -1)
     later = lax.ppermute(cotangent, TIME, [(i + 1, i) for i in range(7)])
-    upward, state_grad, time_cot = states(cotangent, up_weight)
-    later, time_cot = lax.optimization_barrier((later, time_cot))
-    later_up, later_cot = later_states(later, up_weight)
+    upward = own_upward(cotangent)
+    later, upward = lax.optimization_barrier((later, upward))
+    later_up, state_grad, time_cot, later_cot = states(later, upward, up_weight)
     low, high, later_cot = halo(tile, later_cot)
     core = lax.axis_index("core").astype(jnp.int32).reshape(1)
-    activated, pre_grad, mine_one, other_one = forward(
-        core, tile, low, high, spatial_weight, time_cot, later_cot, time_weight
+    pre_grad, mine, other = gradients(
+        core, tile, low, high, spatial_weight, time_cot, later_cot, upward, later_up, time_weight
     )
-    other_one = lax.ppermute(other_one, "core", [(0, 1), (1, 0)])
-    mine_two, other_two = rest(
-        core, tile, high, pre_grad, activated, time_cot, later_cot, upward, later_up, time_weight
-    )
-    other_one, other_two = lax.optimization_barrier((other_one, other_two))
-    other_two = lax.ppermute(other_two, "core", [(0, 1), (1, 0)])
-    value = swap_sum(mine_one, mine_two, other_one, other_two)
+    other = lax.ppermute(other, "core", [(0, 1), (1, 0)])
+    value = swap_sum(mine, other)
     pre_tile = pre_grad.reshape(FRAMES, ROWS, W, C)
     held, value = lax.optimization_barrier((pre_tile, value))
     value = lax.all_to_all(value.reshape(16, 16, 16, 128), PLANE, 0, 0)

time: 89.4 us -> 86.4 us (0.966)
  starting transfers between devices: 33.6 us -> 30.5 us
  waiting for transfers between devices: 15.1 us -> 17.3 us
  local copies, waits for them, and re-layouts: 3.01 us -> 1.98 us
    ppermute x2 -> x1, starting transfers between devices: 4.57 us -> 2.3 us  [local(): other = lax.ppermute(other, 'core', [(0, 1), (1, 0)])]
    ppermute x2, waiting for transfers between devices: 2.51 us -> 3.69 us  [halo(): first = lax.ppermute(jnp.where(even, bottom, top), SPACE, pairs[0])]
    unnamed x13 -> x11, local copies, waits for them, and re-layouts: 3.01 us -> 1.98 us
    pallas_call x9 -> x8, Pallas kernels: 6.56 us -> 6.09 us  [call(): pl.pallas_call(kernel, out_shape=outs, compiler_params=pltpu.CompilerPara...]
    ppermute x2 -> x1, waiting for transfers between devices: 1.94 us -> 2.26 us  [local(): other = lax.ppermute(other, 'core', [(0, 1), (1, 0)])]
  transfers between devices with their start and end apart: 8 -> 7, of which waited for: 5 -> 4; matrix products, arithmetic and copies ran while one was open for 1% -> 1% of each run, Pallas kernels for 4% -> 2%
where the time goes in v1:
time: 86.4 us; the launch traced here: 85.9 us
  starting transfers between devices  30.5 us (35%)
  blocking collectives  29 us (34%)
  waiting for transfers between devices  17.3 us (20%)
  Pallas kernels  6.09 us (7%)
  local copies, waits for them, and re-layouts  1.98 us (2%)
  between operations  0.87 us (1%)
    all_to_all x1, blocking collectives, local(): value = lax.all_to_all(value, 'z', 0, 0)  15 us
    all_to_all x1, blocking collectives, local(): lax.all_to_all(value, GROUP, 0, 0)  14 us
    all_to_all x1, starting transfers between devices, local(): value = lax.all_to_all(value.reshape(16, 16, 16, 128), PLANE, 0, 0)  12.7 us
    all_to_all x1, waiting for transfers between devices, local(): value = lax.all_to_all(value.reshape(16, 16, 16, 128), PLANE, 0, 0)  11.3 us
    ppermute x1, starting transfers between devices, local(): later = lax.ppermute(cotangent, TIME, [(i + 1, i) for i in range(7)])  8.92 us
    pallas_call x8, Pallas kernels, call(): pl.pallas_call(kernel, out_shape=outs, compiler_params=pltpu.CompilerPara...  6.09 us
    ppermute x2, starting transfers between devices, halo(): first = lax.ppermute(jnp.where(even, bottom, top), SPACE, pairs[0])  5.27 us
    ppermute x2, waiting for transfers between devices, halo(): first = lax.ppermute(jnp.where(even, bottom, top), SPACE, pairs[0])  3.69 us
  transfers between devices with their start and end apart: 7, of which 4 were waited for; matrix products, arithmetic and copies ran while one was open for 1% of the time, Pallas kernels for 2%

profile of v1, /device:TPU:1, one launch (start us, length us, event | category | flops | bytes accessed | tf_op | source)
XLA Modules:
  0.0 85.9 jit_solution(723403244784668037)
XLA Ops:
  0.6 0.0 copy-start.1
  0.6 8.9 %collective-permute-start.2 = (bf16[4,4,128,128]{3,2,1,0:T(8,128)(2,1)}, bf16[4,4,128,128]{3,2,1,0:T(8,128)(2,1)S(1)}, u32[]{:S(2)}, u32[]{:S(2)}) collective-permute-start(bf16[4,4,128,128]{3,2,1,0:T(8,128)(2,1)} %bitcast.24), channel_id=1, source_target_pairs={{32,0},{64,32},{96,64},{128,96},{160,128},{192,160},{224,192},{33,... | collective-permute-start | bytes 1572872 | tf_op jit(solution)/shard_map/ppermute | solution.py:295
  9.6 0.9 %copy.20 = bf16[1,2,2,64,256]{4,3,1,2,0:T(8,128)(2,1)S(1)} copy(bf16[1,2,2,64,256]{4,3,2,1,0:T(8,128)(2,1)} %param.5) | data formatting | bytes 262144 | tf_op args[0]
  10.5 0.7 collective-permute-start.1
  11.2 1.9 %collective-permute-start = (bf16[2,64,256]{2,1,0:T(8,128)(2,1)S(1)}, bf16[2,64,256]{2,1,0:T(8,128)(2,1)S(1)}, u32[]{:S(2)}, u32[]{:S(2)}) collective-permute-start(bf16[2,64,256]{2,1,0:T(8,128)(2,1)S(1)} %get-tuple-element.55), channel_id=1, source_target_pairs={{0,1},{2,3},{4,5},{6,7},{8,9},{10,11},{12,13},{14,15},{16,17},{18,... | collective-permute-start | bytes 196616 | tf_op jit(solution)/shard_map/ppermute | solution.py:286
  13.1 0.0 copy-start.2
  13.1 1.0 %copy-done.2 = bf16[1,4,4,128,128]{4,3,2,1,0:T(8,128)(2,1)S(1)} copy-done((bf16[1,4,4,128,128]{4,3,2,1,0:T(8,128)(2,1)S(1)}, bf16[1,4,4,128,128]{4,3,2,1,0:T(8,128)(2,1)}, u32[]{:S(2)}) %copy-start.2) | copy-done | bytes 524312
  14.2 0.3 shard_map.84.up_ref
  14.5 0.0 copy-start
  14.5 0.0 copy-start.3
  14.5 0.0 copy-start.4
  14.5 0.0 collective-permute-done.2.cot_ref
  14.5 0.0 copy-done.1
  14.5 0.6 shard_map.85
  15.1 0.0 collective-permute-done.1
  15.1 1.8 %collective-permute-done = bf16[2,64,256]{2,1,0:T(8,128)(2,1)S(1)} collective-permute-done((bf16[2,64,256]{2,1,0:T(8,128)(2,1)S(1)}, bf16[2,64,256]{2,1,0:T(8,128)(2,1)S(1)}, u32[]{:S(2)}, u32[]{:S(2)}) %collective-permute-start) | collective-permute-done | bytes 65568 | tf_op jit(solution)/shard_map/ppermute | solution.py:286
  16.9 0.0 copy-done
  16.9 0.0 copy-done.3
  16.9 0.0 copy-done.4
  16.9 2.1 %shard_map.86 = (bf16[256,256]{1,0:T(8,128)(2,1)S(1)}, bf16[8,32,16,128]{3,2,1,0:T(8,128)(2,1)S(1)}, bf16[8,32,16,128]{3,2,1,0:T(8,128)(2,1)S(1)}) custom-call(s32[1]{0:T(128)} %bitcast.core_ref, bf16[2,2,64,256]{3,2,1,0:T(8,128)(2,1)S(1)} %bitcast.26, bf16[2,64,256]{2,1,0:T(8,128)(2,1)S(1)} %get-tuple-element.53.low_ref, ...), custom_call_target="tpu_custom_call" | custom-call | flops 1275068416 | bytes 5373956 | tf_op jit(solution)/shard_map/pallas_call | solution.py:51
  19.1 2.3 %collective-permute-start.3 = (bf16[8,32,16,128]{3,2,1,0:T(8,128)(2,1)S(1)}, bf16[8,32,16,128]{3,2,1,0:T(8,128)(2,1)S(1)}, u32[]{:S(2)}, u32[]{:S(2)}) collective-permute-start(bf16[8,32,16,128]{3,2,1,0:T(8,128)(2,1)S(1)} %get-tuple-element.36), channel_id=1, source_target_pairs={{0,32},{32,0},{1,33},{33,1},{2,34},{34,2},{3,35},{35,3},{4,36},{36... | collective-permute-start | bytes 3145736 | tf_op jit(solution)/shard_map/ppermute | solution.py:304
  21.4 2.3 %collective-permute-done.3.arrived_ref = bf16[8,32,16,128]{3,2,1,0:T(8,128)(2,1)S(1)} collective-permute-done((bf16[8,32,16,128]{3,2,1,0:T(8,128)(2,1)S(1)}, bf16[8,32,16,128]{3,2,1,0:T(8,128)(2,1)S(1)}, u32[]{:S(2)}, u32[]{:S(2)}) %collective-permute-start.3) | collective-permute-done | bytes 1048608 | tf_op jit(solution)/shard_map/ppermute | solution.py:304
  23.7 1.1 %shard_map.87 = bf16[8,32,16,128]{3,2,1,0:T(8,128)(2,1)} custom-call(bf16[8,32,16,128]{3,2,1,0:T(8,128)(2,1)S(1)} %get-tuple-element.35.mine_ref, bf16[8,32,16,128]{3,2,1,0:T(8,128)(2,1)S(1)} %collective-permute-done.3.arrived_ref), custom_call_target="tpu_custom_call" | custom-call | bytes 3145728 | tf_op jit(solution)/shard_map/pallas_call | solution.py:51
  24.7 12.7 %all-to-all-start = ((bf16[16,16,16,128]{3,2,1,0:T(8,128)(2,1)}), bf16[16,16,16,128]{3,2,1,0:T(8,128)(2,1)S(1)}, u32[]{:S(2)}, u32[]{:S(2)}) async-start(bf16[16,16,16,128]{3,2,1,0:T(8,128)(2,1)} %bitcast.7), calls=%async_computation | async-start | bytes 2097152 | tf_op jit(solution)/shard_map/all_to_all | solution.py:308
  37.5 0.7 collective-permute-start.5
  38.2 3.3 %collective-permute-start.4 = (bf16[2,64,256]{2,1,0:T(8,128)(2,1)S(1)}, bf16[2,64,256]{2,1,0:T(8,128)(2,1)S(1)}, u32[]{:S(2)}, u32[]{:S(2)}) collective-permute-start(bf16[2,64,256]{2,1,0:T(8,128)(2,1)S(1)} %get-tuple-element.51), channel_id=1, source_target_pairs={{0,1},{2,3},{4,5},{6,7},{8,9},{10,11},{12,13},{14,15},{16,17},{18,... | collective-permute-start | bytes 196616 | tf_op jit(solution)/shard_map/ppermute | solution.py:286
  41.5 0.0 collective-permute-done.5
  41.5 1.9 %collective-permute-done.4 = bf16[2,64,256]{2,1,0:T(8,128)(2,1)S(1)} collective-permute-done((bf16[2,64,256]{2,1,0:T(8,128)(2,1)S(1)}, bf16[2,64,256]{2,1,0:T(8,128)(2,1)S(1)}, u32[]{:S(2)}, u32[]{:S(2)}) %collective-permute-start.4) | collective-permute-done | bytes 65568 | tf_op jit(solution)/shard_map/ppermute | solution.py:286
  43.5 1.2 %shard_map.88 = bf16[256,256]{1,0:T(8,128)(2,1)} custom-call(f32[256,256]{1,0:T(8,128)S(1)} %get-tuple-element.40.state_ref, bf16[2,2,64,256]{3,2,1,0:T(8,128)(2,1)S(1)} %bitcast.23, bf16[2,64,256]{2,1,0:T(8,128)(2,1)S(1)} %get-tuple-element.49.low_ref, bf16[2,64,256]{2,1,0:T(8,128)(2,1)S(1)} %get-tuple-element.48.high_ref, bf16[3,3,256,256]{3,2,1,0:T(8,128)(2,1)S(1)} %copy-done), custom_call_target="tpu_custom_call" | custom-call | flops 301989888 | bytes 1835008 | tf_op jit(solution)/shard_map/pallas_call | solution.py:51
  44.7 11.3 %all-to-all-done.parts_ref = bf16[16,16,16,128]{3,2,1,0:T(8,128)(2,1)S(1)} async-done(((bf16[16,16,16,128]{3,2,1,0:T(8,128)(2,1)}), bf16[16,16,16,128]{3,2,1,0:T(8,128)(2,1)S(1)}, u32[]{:S(2)}, u32[]{:S(2)}) %all-to-all-start) | async-done | bytes 1048608 | tf_op jit(solution)/shard_map/all_to_all | solution.py:308
  56.0 0.1 shard_map.89
  56.2 15.0 %all_to_all.15.parts_ref = bf16[16,16,128]{2,1,0:T(8,128)(2,1)S(1)} all-to-all(bf16[16,16,128]{2,1,0:T(8,128)(2,1)S(1)} %shard_map.89), channel_id=1, replica_groups=mesh['y_lo'=2,'x'=4,'core'=2,'y_hi'=2,'z'=16] {'z'}, dimensions={0} | all-to-all | bytes 131072 | tf_op jit(solution)/shard_map/all_to_all | solution.py:313
  71.2 14.0 %all_to_all.16.in_ref = f32[16,16,128]{2,1,0:T(8,128)S(1)} all-to-all(f32[16,16,128]{2,1,0:T(8,128)S(1)} %shard_map.90), channel_id=1, replica_groups=mesh['y_lo'=2,'x'=4,'core'=2,'y_hi'=2,'z'=16] {'y_lo','x','core'}, dimensions={0} | all-to-all | bytes 262144 | tf_op jit(solution)/shard_map/all_to_all | solution.py:315
  85.2 0.7 shard_map.91
  (5 shorter events, 0.1 us)
Async XLA Ops:
  0.6 13.9 %copy-start.1 = (bf16[256,1024]{1,0:T(8,128)(2,1)S(1)}, bf16[256,1024]{1,0:T(8,128)(2,1)}, u32[]{:S(2)}) copy-start(bf16[256,1024]{1,0:T(8,128)(2,1)} %weight_ref.2) | copy-start | bytes 1572868
  0.6 13.9 %collective-permute-start.2 = (bf16[4,4,128,128]{3,2,1,0:T(8,128)(2,1)}, bf16[4,4,128,128]{3,2,1,0:T(8,128)(2,1)S(1)}, u32[]{:S(2)}, u32[]{:S(2)}) collective-permute-start(bf16[4,4,128,128]{3,2,1,0:T(8,128)(2,1)} %bitcast.24), channel_id=1, source_target_pairs={{32,0},{64,32},{96,64},{128,96},{160,128},{192,160},{224,192},{33,... | collective-permute-start | bytes 1572872 | tf_op jit(solution)/shard_map/ppermute | solution.py:295
  10.5 4.6 %collective-permute-start.1 = (bf16[2,64,256]{2,1,0:T(8,128)(2,1)S(1)}, bf16[2,64,256]{2,1,0:T(8,128)(2,1)S(1)}, u32[]{:S(2)}, u32[]{:S(2)}) collective-permute-start(bf16[2,64,256]{2,1,0:T(8,128)(2,1)S(1)} %get-tuple-element.54), channel_id=1, source_target_pairs={{1,2},{3,4},{5,6},{7,8},{9,10},{11,12},{13,14},{15,16},{17,18},{19... | collective-permute-start | bytes 196616 | tf_op jit(solution)/shard_map/ppermute | solution.py:287
  11.2 5.7 %collective-permute-start = (bf16[2,64,256]{2,1,0:T(8,128)(2,1)S(1)}, bf16[2,64,256]{2,1,0:T(8,128)(2,1)S(1)}, u32[]{:S(2)}, u32[]{:S(2)}) collective-permute-start(bf16[2,64,256]{2,1,0:T(8,128)(2,1)S(1)} %get-tuple-element.55), channel_id=1, source_target_pairs={{0,1},{2,3},{4,5},{6,7},{8,9},{10,11},{12,13},{14,15},{16,17},{18,... | collective-permute-start | bytes 196616 | tf_op jit(solution)/shard_map/ppermute | solution.py:286
  13.1 1.0 %copy-start.2 = (bf16[1,4,4,128,128]{4,3,2,1,0:T(8,128)(2,1)S(1)}, bf16[1,4,4,128,128]{4,3,2,1,0:T(8,128)(2,1)}, u32[]{:S(2)}) copy-start(bf16[1,4,4,128,128]{4,3,2,1,0:T(8,128)(2,1)} %param.6) | copy-start | bytes 1572868
  14.5 2.4 %copy-start = (bf16[3,3,256,256]{3,2,1,0:T(8,128)(2,1)S(1)}, bf16[3,3,256,256]{3,2,1,0:T(8,128)(2,1)}, u32[]{:S(2)}) copy-start(bf16[3,3,256,256]{3,2,1,0:T(8,128)(2,1)} %weight_ref.3) | copy-start | bytes 3538948
  14.5 2.4 %copy-start.3 = (bf16[1,2,2,64,256]{4,3,2,1,0:T(8,128)(2,1)S(1)}, bf16[1,2,2,64,256]{4,3,2,1,0:T(8,128)(2,1)}, u32[]{:S(2)}) copy-start(bf16[1,2,2,64,256]{4,3,2,1,0:T(8,128)(2,1)} %param.5) | copy-start | bytes 393220
  14.5 2.4 %copy-start.4 = (bf16[3,256,256]{2,1,0:T(8,128)(2,1)S(1)}, bf16[3,256,256]{2,1,0:T(8,128)(2,1)}, u32[]{:S(2)}) copy-start(bf16[3,256,256]{2,1,0:T(8,128)(2,1)} %time_ref.1) | copy-start | bytes 1179652
  19.1 4.6 %collective-permute-start.3 = (bf16[8,32,16,128]{3,2,1,0:T(8,128)(2,1)S(1)}, bf16[8,32,16,128]{3,2,1,0:T(8,128)(2,1)S(1)}, u32[]{:S(2)}, u32[]{:S(2)}) collective-permute-start(bf16[8,32,16,128]{3,2,1,0:T(8,128)(2,1)S(1)} %get-tuple-element.36), channel_id=1, source_target_pairs={{0,32},{32,0},{1,33},{33,1},{2,34},{34,2},{3,35},{35,3},{4,36},{36... | collective-permute-start | bytes 3145736 | tf_op jit(solution)/shard_map/ppermute | solution.py:304
  24.7 31.3 %all-to-all-start = ((bf16[16,16,16,128]{3,2,1,0:T(8,128)(2,1)}), bf16[16,16,16,128]{3,2,1,0:T(8,128)(2,1)S(1)}, u32[]{:S(2)}, u32[]{:S(2)}) async-start(bf16[16,16,16,128]{3,2,1,0:T(8,128)(2,1)} %bitcast.7), calls=%async_computation | async-start | bytes 2097152 | tf_op jit(solution)/shard_map/all_to_all | solution.py:308
  37.5 4.0 %collective-permute-start.5 = (bf16[2,64,256]{2,1,0:T(8,128)(2,1)S(1)}, bf16[2,64,256]{2,1,0:T(8,128)(2,1)S(1)}, u32[]{:S(2)}, u32[]{:S(2)}) collective-permute-start(bf16[2,64,256]{2,1,0:T(8,128)(2,1)S(1)} %get-tuple-element.50), channel_id=1, source_target_pairs={{1,2},{3,4},{5,6},{7,8},{9,10},{11,12},{13,14},{15,16},{17,18},{19... | collective-permute-start | bytes 196616 | tf_op jit(solution)/shard_map/ppermute | solution.py:287
  38.2 5.3 %collective-permute-start.4 = (bf16[2,64,256]{2,1,0:T(8,128)(2,1)S(1)}, bf16[2,64,256]{2,1,0:T(8,128)(2,1)S(1)}, u32[]{:S(2)}, u32[]{:S(2)}) collective-permute-start(bf16[2,64,256]{2,1,0:T(8,128)(2,1)S(1)} %get-tuple-element.51), channel_id=1, source_target_pairs={{0,1},{2,3},{4,5},{6,7},{8,9},{10,11},{12,13},{14,15},{16,17},{18,... | collective-permute-start | bytes 196616 | tf_op jit(solution)/shard_map/ppermute | solution.py:286

commit v2 on v1

--- a/solution.py
+++ b/solution.py
@@ -7,9 +7,9 @@
 
 epsilon = 1e-06
 TIME = ("x", "core")
-SPACE = ("y_hi", "z")
+SPACE = ("y_hi", "z_hi", "z_lo")
 GROUP = ("y_lo", "x", "core")
-PLANE = ("y_lo", "x", "y_hi")
+NEAR = ("y_lo", "x", "y_hi", "z_lo")
 C = 256
 W = 64
 FRAMES = 2
@@ -188,25 +188,28 @@
 def swap_sum_kernel(mine_ref, arrived_ref, out_ref, held_ref, sems):
     copies = []
     for at in range(8):
-        total = mine_ref[at].astype(f32) + arrived_ref[at].astype(f32)
-        held_ref[at] = total.astype(bf16)
+        total = (mine_ref[at] + arrived_ref[at]).reshape(2, 8, 2, 16, 128)
+        for low in range(2):
+            held_ref[at, :, low] = total[:, :, low]
         copies.append(pltpu.make_async_copy(held_ref.at[at], out_ref.at[at], sems.at[at]))
         copies[-1].start()
     for copy in copies:
         copy.wait()
 
 
-def plane_sum_kernel(parts_ref, out_ref):
+def total_of(parts_ref):
     total = parts_ref[0].astype(f32)
-    for at in range(1, 16):
+    for at in range(1, parts_ref.shape[0]):
         total = total + parts_ref[at].astype(f32)
-    out_ref[...] = total.astype(bf16)
-
-
-def depth_sum_kernel(parts_ref, out_ref):
-    total = parts_ref[0].astype(f32)
-    for at in range(1, 16):
-        total = total + parts_ref[at].astype(f32)
+    return total
+
+
+def near_sum_kernel(parts_ref, out_ref):
+    out_ref[...] = total_of(parts_ref).astype(bf16)
+
+
+def far_sum_kernel(parts_ref, out_ref):
+    total = total_of(parts_ref)
     for at in range(MEMBERS):
         out_ref[at] = total
 
@@ -257,7 +260,7 @@
 
 
 def swap_sum(*operands):
-    out = shape((8, SPACES, 16, 128), bf16)
+    out = shape((8, 2, 2, 8, 16, 128), bf16)
     return call(
         swap_sum_kernel,
         out,
@@ -305,13 +308,13 @@
     value = swap_sum(mine, other)
     pre_tile = pre_grad.reshape(FRAMES, ROWS, W, C)
     held, value = lax.optimization_barrier((pre_tile, value))
-    value = lax.all_to_all(value.reshape(16, 16, 16, 128), PLANE, 0, 0)
+    value = lax.all_to_all(value.reshape(32, 8, 16, 128), NEAR, 0, 0)
     pre_low, pre_high, state_grad = halo(held, state_grad)
     input_grad = input_gradient(state_grad, pre_tile, pre_low, pre_high, spatial_weight)
     value, input_grad = lax.optimization_barrier((value, input_grad))
-    value = call(plane_sum_kernel, (shape((16, 16, 128), bf16),), 0, value)[0]
-    value = lax.all_to_all(value, "z", 0, 0)
-    value = call(depth_sum_kernel, (shape((MEMBERS, 16, 128), f32),), 0, value)[0]
+    value = call(near_sum_kernel, (shape((8, 16, 128), bf16),), 0, value)[0]
+    value = lax.all_to_all(value, "z_hi", 0, 0)
+    value = call(far_sum_kernel, (shape((MEMBERS, 16, 128), f32),), 0, value)[0]
     spatial_grad, time_grad, up_grad = unpacked(lax.all_to_all(value, GROUP, 0, 0))
     return (
         input_grad.reshape(inputs.shape),
@@ -322,7 +325,9 @@
 
 
 def solution(mesh):
-    whole = Mesh(mesh.devices.reshape(2, 4, 2, 2, 16), ("y_lo", "x", "core", "y_hi", "z"))
+    whole = Mesh(
+        mesh.devices.reshape(2, 4, 2, 2, 8, 2), ("y_lo", "x", "core", "y_hi", "z_hi", "z_lo")
+    )
     tile = P("y_lo", TIME, SPACE, None, None)
     return jax.shard_map(
         local,

time: 86.4 us -> 86.4 us (level)
  waiting for transfers between devices: 17.3 us -> 14.4 us
  blocking collectives: 29 us -> 30.6 us
  starting transfers between devices: 30.5 us -> 31.9 us
    all_to_all x1, waiting for transfers between devices: 11.3 us -> 1.4 us  [local(): value = lax.all_to_all(value.reshape(32, 8, 16, 128), NEAR, 0, 0)]
    ppermute x2, waiting for transfers between devices: 3.69 us -> 10.8 us  [halo(): first = lax.ppermute(jnp.where(even, bottom, top), SPACE, pairs[0])]
    all_to_all x1, blocking collectives: 15 us -> 17.9 us  [local(): value = lax.all_to_all(value, 'z_hi', 0, 0)]
    all_to_all x1, blocking collectives: 14 us -> 12.8 us  [local(): lax.all_to_all(value, GROUP, 0, 0)]
    ppermute x2, starting transfers between devices: 5.27 us -> 6.31 us  [halo(): first = lax.ppermute(jnp.where(even, bottom, top), SPACE, pairs[0])]
where the time goes in v2:
time: 86.4 us; the launch traced here: 85.9 us
  starting transfers between devices  31.9 us (37%)
  blocking collectives  30.6 us (35%)
  waiting for transfers between devices  14.4 us (17%)
  Pallas kernels  6.09 us (7%)
  local copies, waits for them, and re-layouts  1.98 us (2%)
  between operations  0.87 us (1%)
    all_to_all x1, blocking collectives, local(): value = lax.all_to_all(value, 'z_hi', 0, 0)  17.9 us
    all_to_all x1, starting transfers between devices, local(): value = lax.all_to_all(value.reshape(32, 8, 16, 128), NEAR, 0, 0)  13 us
    all_to_all x1, blocking collectives, local(): lax.all_to_all(value, GROUP, 0, 0)  12.8 us
    ppermute x2, waiting for transfers between devices, halo(): first = lax.ppermute(jnp.where(even, bottom, top), SPACE, pairs[0])  10.8 us
    ppermute x1, starting transfers between devices, local(): later = lax.ppermute(cotangent, TIME, [(i + 1, i) for i in range(7)])  8.92 us
    ppermute x2, starting transfers between devices, halo(): first = lax.ppermute(jnp.where(even, bottom, top), SPACE, pairs[0])  6.31 us
    pallas_call x8, Pallas kernels, call(): pl.pallas_call(kernel, out_shape=outs, compiler_params=pltpu.CompilerPara...  6.09 us
    ppermute x1, starting transfers between devices, local(): other = lax.ppermute(other, 'core', [(0, 1), (1, 0)])  2.3 us
  transfers between devices with their start and end apart: 7, of which 4 were waited for; matrix products, arithmetic and copies ran while one was open for 1% of the time, Pallas kernels for 2%

profile of v2, /device:TPU:1, one launch (start us, length us, event | category | flops | bytes accessed | tf_op | source)
XLA Modules:
  0.0 85.9 jit_solution(14984439212545387701)
XLA Ops:
  0.6 0.0 copy-start.1
  0.6 8.9 %collective-permute-start.2 = (bf16[4,4,128,128]{3,2,1,0:T(8,128)(2,1)}, bf16[4,4,128,128]{3,2,1,0:T(8,128)(2,1)S(1)}, u32[]{:S(2)}, u32[]{:S(2)}) collective-permute-start(bf16[4,4,128,128]{3,2,1,0:T(8,128)(2,1)} %bitcast.24), channel_id=1, source_target_pairs={{32,0},{64,32},{96,64},{128,96},{160,128},{192,160},{224,192},{33,... | collective-permute-start | bytes 1572872 | tf_op jit(solution)/shard_map/ppermute | solution.py:298
  9.6 0.9 %copy.20 = bf16[1,2,2,64,256]{4,3,1,2,0:T(8,128)(2,1)S(1)} copy(bf16[1,2,2,64,256]{4,3,2,1,0:T(8,128)(2,1)} %param.5) | data formatting | bytes 262144 | tf_op args[0]
  10.5 0.7 collective-permute-start.1
  11.2 1.9 %collective-permute-start = (bf16[2,64,256]{2,1,0:T(8,128)(2,1)S(1)}, bf16[2,64,256]{2,1,0:T(8,128)(2,1)S(1)}, u32[]{:S(2)}, u32[]{:S(2)}) collective-permute-start(bf16[2,64,256]{2,1,0:T(8,128)(2,1)S(1)} %get-tuple-element.55), channel_id=1, source_target_pairs={{0,1},{2,3},{4,5},{6,7},{8,9},{10,11},{12,13},{14,15},{16,17},{18,... | collective-permute-start | bytes 196616 | tf_op jit(solution)/shard_map/ppermute | solution.py:289
  13.1 0.0 copy-start.2
  13.2 1.0 %copy-done.2 = bf16[1,4,4,128,128]{4,3,2,1,0:T(8,128)(2,1)S(1)} copy-done((bf16[1,4,4,128,128]{4,3,2,1,0:T(8,128)(2,1)S(1)}, bf16[1,4,4,128,128]{4,3,2,1,0:T(8,128)(2,1)}, u32[]{:S(2)}) %copy-start.2) | copy-done | bytes 524312
  14.2 0.3 shard_map.84.up_ref
  14.5 0.0 copy-start
  14.5 0.0 copy-start.3
  14.5 0.0 copy-start.4
  14.5 0.0 collective-permute-done.2.cot_ref
  14.5 0.0 copy-done.1
  14.5 0.6 shard_map.85
  15.1 0.0 collective-permute-done.1
  15.1 1.8 %collective-permute-done = bf16[2,64,256]{2,1,0:T(8,128)(2,1)S(1)} collective-permute-done((bf16[2,64,256]{2,1,0:T(8,128)(2,1)S(1)}, bf16[2,64,256]{2,1,0:T(8,128)(2,1)S(1)}, u32[]{:S(2)}, u32[]{:S(2)}) %collective-permute-start) | collective-permute-done | bytes 65568 | tf_op jit(solution)/shard_map/ppermute | solution.py:289
  16.9 0.0 copy-done
  16.9 0.0 copy-done.3
  16.9 0.0 copy-done.4
  16.9 2.1 %shard_map.86 = (bf16[256,256]{1,0:T(8,128)(2,1)S(1)}, bf16[8,32,16,128]{3,2,1,0:T(8,128)(2,1)S(1)}, bf16[8,32,16,128]{3,2,1,0:T(8,128)(2,1)S(1)}) custom-call(s32[1]{0:T(128)} %bitcast.core_ref, bf16[2,2,64,256]{3,2,1,0:T(8,128)(2,1)S(1)} %bitcast.26, bf16[2,64,256]{2,1,0:T(8,128)(2,1)S(1)} %get-tuple-element.53.low_ref, ...), custom_call_target="tpu_custom_call" | custom-call | flops 1275068416 | bytes 5373956 | tf_op jit(solution)/shard_map/pallas_call | solution.py:51
  19.1 2.3 %collective-permute-start.3 = (bf16[8,32,16,128]{3,2,1,0:T(8,128)(2,1)S(1)}, bf16[8,32,16,128]{3,2,1,0:T(8,128)(2,1)S(1)}, u32[]{:S(2)}, u32[]{:S(2)}) collective-permute-start(bf16[8,32,16,128]{3,2,1,0:T(8,128)(2,1)S(1)} %get-tuple-element.36), channel_id=1, source_target_pairs={{0,32},{32,0},{1,33},{33,1},{2,34},{34,2},{3,35},{35,3},{4,36},{36... | collective-permute-start | bytes 3145736 | tf_op jit(solution)/shard_map/ppermute | solution.py:307
  21.4 2.3 %collective-permute-done.3.arrived_ref = bf16[8,32,16,128]{3,2,1,0:T(8,128)(2,1)S(1)} collective-permute-done((bf16[8,32,16,128]{3,2,1,0:T(8,128)(2,1)S(1)}, bf16[8,32,16,128]{3,2,1,0:T(8,128)(2,1)S(1)}, u32[]{:S(2)}, u32[]{:S(2)}) %collective-permute-start.3) | collective-permute-done | bytes 1048608 | tf_op jit(solution)/shard_map/ppermute | solution.py:307
  23.7 1.1 %shard_map.87 = bf16[8,2,2,8,16,128]{5,4,3,2,1,0:T(8,128)(2,1)} custom-call(bf16[8,32,16,128]{3,2,1,0:T(8,128)(2,1)S(1)} %get-tuple-element.35.mine_ref, bf16[8,32,16,128]{3,2,1,0:T(8,128)(2,1)S(1)} %collective-permute-done.3.arrived_ref), custom_call_target="tpu_custom_call" | custom-call | bytes 3145728 | tf_op jit(solution)/shard_map/pallas_call | solution.py:51
  24.8 13.0 %all-to-all-start = ((bf16[32,8,16,128]{3,2,1,0:T(8,128)(2,1)}), bf16[32,8,16,128]{3,2,1,0:T(8,128)(2,1)S(1)}, u32[]{:S(2)}, u32[]{:S(2)}) async-start(bf16[32,8,16,128]{3,2,1,0:T(8,128)(2,1)} %bitcast.7), calls=%async_computation | async-start | bytes 2097152 | tf_op jit(solution)/shard_map/all_to_all | solution.py:311
  37.8 0.7 collective-permute-start.5
  38.5 4.4 %collective-permute-start.4 = (bf16[2,64,256]{2,1,0:T(8,128)(2,1)S(1)}, bf16[2,64,256]{2,1,0:T(8,128)(2,1)S(1)}, u32[]{:S(2)}, u32[]{:S(2)}) collective-permute-start(bf16[2,64,256]{2,1,0:T(8,128)(2,1)S(1)} %get-tuple-element.51), channel_id=1, source_target_pairs={{0,1},{2,3},{4,5},{6,7},{8,9},{10,11},{12,13},{14,15},{16,17},{18,... | collective-permute-start | bytes 196616 | tf_op jit(solution)/shard_map/ppermute | solution.py:289
  42.9 0.0 collective-permute-done.5
  42.9 9.0 %collective-permute-done.4 = bf16[2,64,256]{2,1,0:T(8,128)(2,1)S(1)} collective-permute-done((bf16[2,64,256]{2,1,0:T(8,128)(2,1)S(1)}, bf16[2,64,256]{2,1,0:T(8,128)(2,1)S(1)}, u32[]{:S(2)}, u32[]{:S(2)}) %collective-permute-start.4) | collective-permute-done | bytes 65568 | tf_op jit(solution)/shard_map/ppermute | solution.py:289
  51.9 1.2 %shard_map.88 = bf16[256,256]{1,0:T(8,128)(2,1)} custom-call(f32[256,256]{1,0:T(8,128)S(1)} %get-tuple-element.40.state_ref, bf16[2,2,64,256]{3,2,1,0:T(8,128)(2,1)S(1)} %bitcast.23, bf16[2,64,256]{2,1,0:T(8,128)(2,1)S(1)} %get-tuple-element.49.low_ref, bf16[2,64,256]{2,1,0:T(8,128)(2,1)S(1)} %get-tuple-element.48.high_ref, bf16[3,3,256,256]{3,2,1,0:T(8,128)(2,1)S(1)} %copy-done), custom_call_target="tpu_custom_call" | custom-call | flops 301989888 | bytes 1835008 | tf_op jit(solution)/shard_map/pallas_call | solution.py:51
  53.1 1.4 %all-to-all-done.parts_ref = bf16[32,8,16,128]{3,2,1,0:T(8,128)(2,1)S(1)} async-done(((bf16[32,8,16,128]{3,2,1,0:T(8,128)(2,1)}), bf16[32,8,16,128]{3,2,1,0:T(8,128)(2,1)S(1)}, u32[]{:S(2)}, u32[]{:S(2)}) %all-to-all-start) | async-done | bytes 1048608 | tf_op jit(solution)/shard_map/all_to_all | solution.py:311
  54.5 0.1 shard_map.89
  54.6 17.9 %all_to_all.15.parts_ref = bf16[8,16,128]{2,1,0:T(8,128)(2,1)S(1)} all-to-all(bf16[8,16,128]{2,1,0:T(8,128)(2,1)S(1)} %shard_map.89), channel_id=1, replica_groups=mesh['y_lo'=2,'x'=4,'core'=2,'y_hi'=2,'z_hi'=8,'z_lo'=2] {'z_hi'}, dimensions={0} | all-to-all | bytes 65536 | tf_op jit(solution)/shard_map/all_to_all | solution.py:316
  72.5 12.8 %all_to_all.16.in_ref = f32[16,16,128]{2,1,0:T(8,128)S(1)} all-to-all(f32[16,16,128]{2,1,0:T(8,128)S(1)} %shard_map.90), channel_id=1, replica_groups=mesh['y_lo'=2,'x'=4,'core'=2,'y_hi'=2,'z_hi'=8,'z_lo'=2] {'y_lo','x','co..., dimensions={0} | all-to-all | bytes 262144 | tf_op jit(solution)/shard_map/all_to_all | solution.py:318
  85.3 0.7 shard_map.91
  (5 shorter events, 0.1 us)
Async XLA Ops:
  0.6 13.9 %copy-start.1 = (bf16[256,1024]{1,0:T(8,128)(2,1)S(1)}, bf16[256,1024]{1,0:T(8,128)(2,1)}, u32[]{:S(2)}) copy-start(bf16[256,1024]{1,0:T(8,128)(2,1)} %weight_ref.2) | copy-start | bytes 1572868
  0.6 13.9 %collective-permute-start.2 = (bf16[4,4,128,128]{3,2,1,0:T(8,128)(2,1)}, bf16[4,4,128,128]{3,2,1,0:T(8,128)(2,1)S(1)}, u32[]{:S(2)}, u32[]{:S(2)}) collective-permute-start(bf16[4,4,128,128]{3,2,1,0:T(8,128)(2,1)} %bitcast.24), channel_id=1, source_target_pairs={{32,0},{64,32},{96,64},{128,96},{160,128},{192,160},{224,192},{33,... | collective-permute-start | bytes 1572872 | tf_op jit(solution)/shard_map/ppermute | solution.py:298
  10.5 4.6 %collective-permute-start.1 = (bf16[2,64,256]{2,1,0:T(8,128)(2,1)S(1)}, bf16[2,64,256]{2,1,0:T(8,128)(2,1)S(1)}, u32[]{:S(2)}, u32[]{:S(2)}) collective-permute-start(bf16[2,64,256]{2,1,0:T(8,128)(2,1)S(1)} %get-tuple-element.54), channel_id=1, source_target_pairs={{1,2},{3,4},{5,6},{7,8},{9,10},{11,12},{13,14},{15,16},{17,18},{19... | collective-permute-start | bytes 196616 | tf_op jit(solution)/shard_map/ppermute | solution.py:290
  11.2 5.7 %collective-permute-start = (bf16[2,64,256]{2,1,0:T(8,128)(2,1)S(1)}, bf16[2,64,256]{2,1,0:T(8,128)(2,1)S(1)}, u32[]{:S(2)}, u32[]{:S(2)}) collective-permute-start(bf16[2,64,256]{2,1,0:T(8,128)(2,1)S(1)} %get-tuple-element.55), channel_id=1, source_target_pairs={{0,1},{2,3},{4,5},{6,7},{8,9},{10,11},{12,13},{14,15},{16,17},{18,... | collective-permute-start | bytes 196616 | tf_op jit(solution)/shard_map/ppermute | solution.py:289
  13.1 1.0 %copy-start.2 = (bf16[1,4,4,128,128]{4,3,2,1,0:T(8,128)(2,1)S(1)}, bf16[1,4,4,128,128]{4,3,2,1,0:T(8,128)(2,1)}, u32[]{:S(2)}) copy-start(bf16[1,4,4,128,128]{4,3,2,1,0:T(8,128)(2,1)} %param.6) | copy-start | bytes 1572868
  14.5 2.4 %copy-start = (bf16[3,3,256,256]{3,2,1,0:T(8,128)(2,1)S(1)}, bf16[3,3,256,256]{3,2,1,0:T(8,128)(2,1)}, u32[]{:S(2)}) copy-start(bf16[3,3,256,256]{3,2,1,0:T(8,128)(2,1)} %weight_ref.3) | copy-start | bytes 3538948
  14.5 2.4 %copy-start.3 = (bf16[1,2,2,64,256]{4,3,2,1,0:T(8,128)(2,1)S(1)}, bf16[1,2,2,64,256]{4,3,2,1,0:T(8,128)(2,1)}, u32[]{:S(2)}) copy-start(bf16[1,2,2,64,256]{4,3,2,1,0:T(8,128)(2,1)} %param.5) | copy-start | bytes 393220
  14.5 2.4 %copy-start.4 = (bf16[3,256,256]{2,1,0:T(8,128)(2,1)S(1)}, bf16[3,256,256]{2,1,0:T(8,128)(2,1)}, u32[]{:S(2)}) copy-start(bf16[3,256,256]{2,1,0:T(8,128)(2,1)} %time_ref.1) | copy-start | bytes 1179652
  19.1 4.6 %collective-permute-start.3 = (bf16[8,32,16,128]{3,2,1,0:T(8,128)(2,1)S(1)}, bf16[8,32,16,128]{3,2,1,0:T(8,128)(2,1)S(1)}, u32[]{:S(2)}, u32[]{:S(2)}) collective-permute-start(bf16[8,32,16,128]{3,2,1,0:T(8,128)(2,1)S(1)} %get-tuple-element.36), channel_id=1, source_target_pairs={{0,32},{32,0},{1,33},{33,1},{2,34},{34,2},{3,35},{35,3},{4,36},{36... | collective-permute-start | bytes 3145736 | tf_op jit(solution)/shard_map/ppermute | solution.py:307
  24.8 29.7 %all-to-all-start = ((bf16[32,8,16,128]{3,2,1,0:T(8,128)(2,1)}), bf16[32,8,16,128]{3,2,1,0:T(8,128)(2,1)S(1)}, u32[]{:S(2)}, u32[]{:S(2)}) async-start(bf16[32,8,16,128]{3,2,1,0:T(8,128)(2,1)} %bitcast.7), calls=%async_computation | async-start | bytes 2097152 | tf_op jit(solution)/shard_map/all_to_all | solution.py:311
  37.8 5.1 %collective-permute-start.5 = (bf16[2,64,256]{2,1,0:T(8,128)(2,1)S(1)}, bf16[2,64,256]{2,1,0:T(8,128)(2,1)S(1)}, u32[]{:S(2)}, u32[]{:S(2)}) collective-permute-start(bf16[2,64,256]{2,1,0:T(8,128)(2,1)S(1)} %get-tuple-element.50), channel_id=1, source_target_pairs={{1,2},{3,4},{5,6},{7,8},{9,10},{11,12},{13,14},{15,16},{17,18},{19... | collective-permute-start | bytes 196616 | tf_op jit(solution)/shard_map/ppermute | solution.py:290
  38.5 13.4 %collective-permute-start.4 = (bf16[2,64,256]{2,1,0:T(8,128)(2,1)S(1)}, bf16[2,64,256]{2,1,0:T(8,128)(2,1)S(1)}, u32[]{:S(2)}, u32[]{:S(2)}) collective-permute-start(bf16[2,64,256]{2,1,0:T(8,128)(2,1)S(1)} %get-tuple-element.51), channel_id=1, source_target_pairs={{0,1},{2,3},{4,5},{6,7},{8,9},{10,11},{12,13},{14,15},{16,17},{18,... | collective-permute-start | bytes 196616 | tf_op jit(solution)/shard_map/ppermute | solution.py:289

commit v3 on v2

--- a/solution.py
+++ b/solution.py
@@ -98,13 +98,23 @@
 
 
 def state_kernel(
-    cot_ref, up_ref, weight_ref, later_up_ref, state_ref, time_cot_ref, later_cot_ref
+    cot_ref, up_ref, weight_ref, time_ref, later_up_ref, state_ref, act_grad_ref, time_cot_ref,
+    later_cot_ref,
 ):
     state = state_of(up_ref, weight_ref)
     state_ref[...] = state
     time_cot_ref[...] = state.astype(bf16)
     arranged(cot_ref, later_up_ref)
     later_cot_ref[...] = state_of(later_up_ref, weight_ref).astype(bf16)
+    cots = shifted_cots(time_cot_ref, later_cot_ref)
+    act_grad = dot_bt(cots[0], time_ref[0]) + dot_bt(cots[1], time_ref[1])
+    act_grad_ref[...] = act_grad + dot_bt(cots[2], time_ref[2])
+
+
+def shifted_cots(cot_ref, later_ref):
+    half = ROWS * W
+    middle = jnp.concatenate([cot_ref[half:, :], later_ref[:half, :]], axis=0)
+    return [cot_ref[...], middle, later_ref[...]]
 
 
 def rows_at(block, low, high, offset):
@@ -133,8 +143,8 @@
 
 
 def gradients_kernel(
-    core_ref, in_ref, low_ref, high_ref, spatial_ref, cot_ref, later_cot_ref, up_ref, later_up_ref,
-    time_ref, pre_ref, mine_ref, other_ref,
+    core_ref, in_ref, low_ref, high_ref, spatial_ref, act_grad_ref, cot_ref, later_cot_ref, up_ref,
+    later_up_ref, time_ref, pre_ref, mine_ref, other_ref,
 ):
     half = ROWS * W
     taps = [None] * 3
@@ -148,9 +158,7 @@
     normed = pre_act / scale
     sig = 1.0 / (1.0 + jnp.exp(-normed))
     act = (normed / (1.0 + jnp.exp(-normed))).astype(bf16)
-    middle = jnp.concatenate([cot_ref[half:, :], later_cot_ref[:half, :]], axis=0)
-    act_grad = dot_bt(cot_ref[...], time_ref[0]) + dot_bt(middle, time_ref[1])
-    act_grad = act_grad + dot_bt(later_cot_ref[...], time_ref[2])
+    act_grad = act_grad_ref[...]
     norm_grad = act_grad * sig * (1.0 + normed * (1.0 - sig))
     mean = jnp.mean(norm_grad * normed, -1, keepdims=True)
     pre = ((norm_grad - normed * mean) / scale).astype(bf16)
@@ -158,7 +166,7 @@
     wide = pre.astype(f32)
     shifted = [from_right(wide).astype(bf16), pre, from_left(wide).astype(bf16)]
 
-    cots = [cot_ref[...], middle, later_cot_ref[...]]
+    cots = shifted_cots(cot_ref, later_cot_ref)
 
     def tap(at):
         if at < 9:
@@ -246,10 +254,10 @@
     return call(own_kernel, (shape((4, PIX, C), bf16),), 2 * PIX * C * C, cotangent)[0]
 
 
-def states(later, upward, up_weight):
-    flat = shape((PIX, C), bf16)
-    outs = (shape((4, PIX, C), bf16), shape((PIX, C), f32), flat, flat)
-    return call(state_kernel, outs, 18 * PIX * C * C, later, upward, up_weight)
+def states(*operands):
+    wide, flat = shape((PIX, C), f32), shape((PIX, C), bf16)
+    outs = (shape((4, PIX, C), bf16), wide, wide, flat, flat)
+    return call(state_kernel, outs, 24 * PIX * C * C, *operands)
 
 
 def gradients(*operands):
@@ -298,11 +306,14 @@
     later = lax.ppermute(cotangent, TIME, [(i + 1, i) for i in range(7)])
     upward = own_upward(cotangent)
     later, upward = lax.optimization_barrier((later, upward))
-    later_up, state_grad, time_cot, later_cot = states(later, upward, up_weight)
+    later_up, state_grad, act_grad, time_cot, later_cot = states(
+        later, upward, up_weight, time_weight
+    )
     low, high, later_cot = halo(tile, later_cot)
     core = lax.axis_index("core").astype(jnp.int32).reshape(1)
     pre_grad, mine, other = gradients(
-        core, tile, low, high, spatial_weight, time_cot, later_cot, upward, later_up, time_weight
+        core, tile, low, high, spatial_weight, act_grad, time_cot, later_cot, upward, later_up,
+        time_weight,
     )
     other = lax.ppermute(other, "core", [(0, 1), (1, 0)])
     value = swap_sum(mine, other)
@@ -311,9 +322,9 @@
     value = lax.all_to_all(value.reshape(32, 8, 16, 128), NEAR, 0, 0)
     pre_low, pre_high, state_grad = halo(held, state_grad)
     input_grad = input_gradient(state_grad, pre_tile, pre_low, pre_high, spatial_weight)
-    value, input_grad = lax.optimization_barrier((value, input_grad))
     value = call(near_sum_kernel, (shape((8, 16, 128), bf16),), 0, value)[0]
     value = lax.all_to_all(value, "z_hi", 0, 0)
+    value, input_grad = lax.optimization_barrier((value, input_grad))
     value = call(far_sum_kernel, (shape((MEMBERS, 16, 128), f32),), 0, value)[0]
     spatial_grad, time_grad, up_grad = unpacked(lax.all_to_all(value, GROUP, 0, 0))
     return (

time: 86.4 us -> 87.4 us (1.012)
  blocking collectives: 30.6 us -> 12.8 us
  waiting for transfers between devices: 14.4 us -> 25.2 us
  starting transfers between devices: 31.9 us -> 38.2 us
  Pallas kernels: 6.09 us -> 7.13 us
    all_to_all x1 -> x0, blocking collectives: 17.9 us -> none  [local(): value = lax.all_to_all(value, 'z_hi', 0, 0)]
    all_to_all x0 -> x1, waiting for transfers between devices: none -> 10.6 us  [local(): value = lax.all_to_all(value, 'z_hi', 0, 0)]
    all_to_all x0 -> x1, starting transfers between devices: none -> 6.06 us  [local(): value = lax.all_to_all(value, 'z_hi', 0, 0)]
    all_to_all x1, waiting for transfers between devices: 1.4 us -> 2.59 us  [local(): value = lax.all_to_all(value.reshape(32, 8, 16, 128), NEAR, 0, 0)]
    pallas_call x8, Pallas kernels: 6.09 us -> 7.13 us  [call(): pl.pallas_call(kernel, out_shape=outs, compiler_params=pltpu.CompilerPara...]
    ppermute x2, waiting for transfers between devices: 10.8 us -> 9.77 us  [halo(): first = lax.ppermute(jnp.where(even, bottom, top), SPACE, pairs[0])]
  transfers between devices with their start and end apart: 7 -> 8, of which waited for: 4 -> 5; matrix products, arithmetic and copies ran while one was open for 1% -> 1% of each run, Pallas kernels for 2% -> 3%
where the time goes in v3:
time: 87.4 us; the launch traced here: 86.8 us
  starting transfers between devices  38.2 us (44%)
  waiting for transfers between devices  25.2 us (29%)
  blocking collectives  12.8 us (15%)
  Pallas kernels  7.13 us (8%)
  local copies, waits for them, and re-layouts  2.63 us (3%)
    all_to_all x1, starting transfers between devices, local(): value = lax.all_to_all(value.reshape(32, 8, 16, 128), NEAR, 0, 0)  13.2 us
    all_to_all x1, blocking collectives, local(): lax.all_to_all(value, GROUP, 0, 0)  12.8 us
    all_to_all x1, waiting for transfers between devices, local(): value = lax.all_to_all(value, 'z_hi', 0, 0)  10.6 us
    ppermute x2, waiting for transfers between devices, halo(): first = lax.ppermute(jnp.where(even, bottom, top), SPACE, pairs[0])  9.77 us
    ppermute x1, starting transfers between devices, local(): later = lax.ppermute(cotangent, TIME, [(i + 1, i) for i in range(7)])  8.92 us
    pallas_call x8, Pallas kernels, call(): pl.pallas_call(kernel, out_shape=outs, compiler_params=pltpu.CompilerPara...  7.13 us
    ppermute x2, starting transfers between devices, halo(): first = lax.ppermute(jnp.where(even, bottom, top), SPACE, pairs[0])  6.31 us
    all_to_all x1, starting transfers between devices, local(): value = lax.all_to_all(value, 'z_hi', 0, 0)  6.06 us
  transfers between devices with their start and end apart: 8, of which 5 were waited for; matrix products, arithmetic and copies ran while one was open for 1% of the time, Pallas kernels for 3%

profile of v3, /device:TPU:1, one launch (start us, length us, event | category | flops | bytes accessed | tf_op | source)
XLA Modules:
  0.0 86.8 jit_solution(17758303201145877856)
XLA Ops:
  0.6 0.0 copy-start.2
  0.6 8.9 %collective-permute-start.2 = (bf16[4,4,128,128]{3,2,1,0:T(8,128)(2,1)}, bf16[4,4,128,128]{3,2,1,0:T(8,128)(2,1)S(1)}, u32[]{:S(2)}, u32[]{:S(2)}) collective-permute-start(bf16[4,4,128,128]{3,2,1,0:T(8,128)(2,1)} %bitcast.24), channel_id=1, source_target_pairs={{32,0},{64,32},{96,64},{128,96},{160,128},{192,160},{224,192},{33,... | collective-permute-start | bytes 1572872 | tf_op jit(solution)/shard_map/ppermute | solution.py:306
  9.6 0.9 %copy.20 = bf16[1,2,2,64,256]{4,3,1,2,0:T(8,128)(2,1)S(1)} copy(bf16[1,2,2,64,256]{4,3,2,1,0:T(8,128)(2,1)} %param.5) | data formatting | bytes 262144 | tf_op args[0]
  10.5 0.7 collective-permute-start.1
  11.2 1.9 %collective-permute-start = (bf16[2,64,256]{2,1,0:T(8,128)(2,1)S(1)}, bf16[2,64,256]{2,1,0:T(8,128)(2,1)S(1)}, u32[]{:S(2)}, u32[]{:S(2)}) collective-permute-start(bf16[2,64,256]{2,1,0:T(8,128)(2,1)S(1)} %get-tuple-element.57), channel_id=1, source_target_pairs={{0,1},{2,3},{4,5},{6,7},{8,9},{10,11},{12,13},{14,15},{16,17},{18,... | collective-permute-start | bytes 196616 | tf_op jit(solution)/shard_map/ppermute | solution.py:297
  13.1 0.0 copy-start.1
  13.2 1.0 %copy-done.1 = bf16[1,4,4,128,128]{4,3,2,1,0:T(8,128)(2,1)S(1)} copy-done((bf16[1,4,4,128,128]{4,3,2,1,0:T(8,128)(2,1)S(1)}, bf16[1,4,4,128,128]{4,3,2,1,0:T(8,128)(2,1)}, u32[]{:S(2)}) %copy-start.1) | copy-done | bytes 524312
  14.2 0.0 copy-start.3
  14.2 0.3 shard_map.84.up_ref
  14.5 0.0 copy-start
  14.5 0.0 copy-start.4
  14.5 0.0 collective-permute-done.2.cot_ref
  14.5 0.0 copy-done.2
  14.5 0.7 copy-done.3
  15.2 0.9 %shard_map.85 = (bf16[4,256,256]{2,1,0:T(8,128)(2,1)S(1)}, f32[256,256]{1,0:T(8,128)S(1)}, f32[256,256]{1,0:T(8,128)S(1)}, bf16[256,256]{1,0:T(8,128)(2,1)S(1)}, bf16[256,256]{1,0:T(8,128)(2,1)S(1)}) custom-call(bf16[4,4,128,128]{3,2,1,0:T(8,128)(2,1)S(1)} %collective-permute-done.2.cot_ref, bf16[4,256,256]{2,1,0:T(8,128)(2,1)S(1)} %shard_map.84.up_ref, ...), custom_call_target="tpu_custom_call" | custom-call | flops 402653184 | bytes 3276800 | tf_op jit(solution)/shard_map/pallas_call | solution.py:51
  16.1 0.0 collective-permute-done.1
  16.1 0.8 collective-permute-done
  16.9 0.0 copy-done
  16.9 0.0 copy-done.4
  16.9 2.2 %shard_map.86 = (bf16[256,256]{1,0:T(8,128)(2,1)S(1)}, bf16[8,32,16,128]{3,2,1,0:T(8,128)(2,1)S(1)}, bf16[8,32,16,128]{3,2,1,0:T(8,128)(2,1)S(1)}) custom-call(s32[1]{0:T(128)} %bitcast.core_ref, bf16[2,2,64,256]{3,2,1,0:T(8,128)(2,1)S(1)} %bitcast.26, bf16[2,64,256]{2,1,0:T(8,128)(2,1)S(1)} %get-tuple-element.55.low_ref, ...), custom_call_target="tpu_custom_call" | custom-call | flops 1275068416 | bytes 5636100 | tf_op jit(solution)/shard_map/pallas_call | solution.py:51
  19.1 2.3 %collective-permute-start.3 = (bf16[8,32,16,128]{3,2,1,0:T(8,128)(2,1)S(1)}, bf16[8,32,16,128]{3,2,1,0:T(8,128)(2,1)S(1)}, u32[]{:S(2)}, u32[]{:S(2)}) collective-permute-start(bf16[8,32,16,128]{3,2,1,0:T(8,128)(2,1)S(1)} %get-tuple-element.38), channel_id=1, source_target_pairs={{0,32},{32,0},{1,33},{33,1},{2,34},{34,2},{3,35},{35,3},{4,36},{36... | collective-permute-start | bytes 3145736 | tf_op jit(solution)/shard_map/ppermute | solution.py:318
  21.5 2.3 %collective-permute-done.3.arrived_ref = bf16[8,32,16,128]{3,2,1,0:T(8,128)(2,1)S(1)} collective-permute-done((bf16[8,32,16,128]{3,2,1,0:T(8,128)(2,1)S(1)}, bf16[8,32,16,128]{3,2,1,0:T(8,128)(2,1)S(1)}, u32[]{:S(2)}, u32[]{:S(2)}) %collective-permute-start.3) | collective-permute-done | bytes 1048608 | tf_op jit(solution)/shard_map/ppermute | solution.py:318
  23.7 1.1 %shard_map.87 = bf16[8,2,2,8,16,128]{5,4,3,2,1,0:T(8,128)(2,1)} custom-call(bf16[8,32,16,128]{3,2,1,0:T(8,128)(2,1)S(1)} %get-tuple-element.37.mine_ref, bf16[8,32,16,128]{3,2,1,0:T(8,128)(2,1)S(1)} %collective-permute-done.3.arrived_ref), custom_call_target="tpu_custom_call" | custom-call | bytes 3145728 | tf_op jit(solution)/shard_map/pallas_call | solution.py:51
  24.8 13.2 %all-to-all-start = ((bf16[32,8,16,128]{3,2,1,0:T(8,128)(2,1)}), bf16[32,8,16,128]{3,2,1,0:T(8,128)(2,1)S(1)}, u32[]{:S(2)}, u32[]{:S(2)}) async-start(bf16[32,8,16,128]{3,2,1,0:T(8,128)(2,1)} %bitcast.7), calls=%async_computation | async-start | bytes 2097152 | tf_op jit(solution)/shard_map/all_to_all | solution.py:322
  38.1 0.7 collective-permute-start.5
  38.8 4.4 %collective-permute-start.4 = (bf16[2,64,256]{2,1,0:T(8,128)(2,1)S(1)}, bf16[2,64,256]{2,1,0:T(8,128)(2,1)S(1)}, u32[]{:S(2)}, u32[]{:S(2)}) collective-permute-start(bf16[2,64,256]{2,1,0:T(8,128)(2,1)S(1)} %get-tuple-element.53), channel_id=1, source_target_pairs={{0,1},{2,3},{4,5},{6,7},{8,9},{10,11},{12,13},{14,15},{16,17},{18,... | collective-permute-start | bytes 196616 | tf_op jit(solution)/shard_map/ppermute | solution.py:297
  43.2 0.0 collective-permute-done.5
  43.2 9.0 %collective-permute-done.4 = bf16[2,64,256]{2,1,0:T(8,128)(2,1)S(1)} collective-permute-done((bf16[2,64,256]{2,1,0:T(8,128)(2,1)S(1)}, bf16[2,64,256]{2,1,0:T(8,128)(2,1)S(1)}, u32[]{:S(2)}, u32[]{:S(2)}) %collective-permute-start.4) | collective-permute-done | bytes 65568 | tf_op jit(solution)/shard_map/ppermute | solution.py:297
  52.2 2.6 %all-to-all-done.parts_ref = bf16[32,8,16,128]{3,2,1,0:T(8,128)(2,1)S(1)} async-done(((bf16[32,8,16,128]{3,2,1,0:T(8,128)(2,1)}), bf16[32,8,16,128]{3,2,1,0:T(8,128)(2,1)S(1)}, u32[]{:S(2)}, u32[]{:S(2)}) %all-to-all-start) | async-done | bytes 1048608 | tf_op jit(solution)/shard_map/all_to_all | solution.py:322
  54.8 0.8 shard_map.88
  55.5 6.1 %all-to-all-start.1 = ((bf16[8,16,128]{2,1,0:T(8,128)(2,1)}), bf16[8,16,128]{2,1,0:T(8,128)(2,1)S(1)}, u32[]{:S(2)}, u32[]{:S(2)}) async-start(bf16[8,16,128]{2,1,0:T(8,128)(2,1)} %shard_map.88), calls=%async_computation.1 | async-start | bytes 65536 | tf_op jit(solution)/shard_map/all_to_all | solution.py:326
  61.6 1.2 %shard_map.89 = bf16[256,256]{1,0:T(8,128)(2,1)} custom-call(f32[256,256]{1,0:T(8,128)S(1)} %get-tuple-element.42.state_ref, bf16[2,2,64,256]{3,2,1,0:T(8,128)(2,1)S(1)} %bitcast.23, bf16[2,64,256]{2,1,0:T(8,128)(2,1)S(1)} %get-tuple-element.51.low_ref, bf16[2,64,256]{2,1,0:T(8,128)(2,1)S(1)} %get-tuple-element.50.high_ref, bf16[3,3,256,256]{3,2,1,0:T(8,128)(2,1)S(1)} %copy-done), custom_call_target="tpu_custom_call" | custom-call | flops 301989888 | bytes 1835008 | tf_op jit(solution)/shard_map/pallas_call | solution.py:51
  62.8 10.6 %all-to-all-done.1.parts_ref = bf16[8,16,128]{2,1,0:T(8,128)(2,1)S(1)} async-done(((bf16[8,16,128]{2,1,0:T(8,128)(2,1)}), bf16[8,16,128]{2,1,0:T(8,128)(2,1)S(1)}, u32[]{:S(2)}, u32[]{:S(2)}) %all-to-all-start.1) | async-done | bytes 32800 | tf_op jit(solution)/shard_map/all_to_all | solution.py:326
  73.4 12.8 %all_to_all.15.in_ref = f32[16,16,128]{2,1,0:T(8,128)S(1)} all-to-all(f32[16,16,128]{2,1,0:T(8,128)S(1)} %shard_map.90), channel_id=1, replica_groups=mesh['y_lo'=2,'x'=4,'core'=2,'y_hi'=2,'z_hi'=8,'z_lo'=2] {'y_lo','x','co..., dimensions={0} | all-to-all | bytes 262144 | tf_op jit(solution)/shard_map/all_to_all | solution.py:329
  86.2 0.7 shard_map.91
  (5 shorter events, 0.1 us)
Async XLA Ops:
  0.6 13.9 %copy-start.2 = (bf16[256,1024]{1,0:T(8,128)(2,1)S(1)}, bf16[256,1024]{1,0:T(8,128)(2,1)}, u32[]{:S(2)}) copy-start(bf16[256,1024]{1,0:T(8,128)(2,1)} %weight_ref.2) | copy-start | bytes 1572868
  0.6 13.9 %collective-permute-start.2 = (bf16[4,4,128,128]{3,2,1,0:T(8,128)(2,1)}, bf16[4,4,128,128]{3,2,1,0:T(8,128)(2,1)S(1)}, u32[]{:S(2)}, u32[]{:S(2)}) collective-permute-start(bf16[4,4,128,128]{3,2,1,0:T(8,128)(2,1)} %bitcast.24), channel_id=1, source_target_pairs={{32,0},{64,32},{96,64},{128,96},{160,128},{192,160},{224,192},{33,... | collective-permute-start | bytes 1572872 | tf_op jit(solution)/shard_map/ppermute | solution.py:306
  10.5 5.6 %collective-permute-start.1 = (bf16[2,64,256]{2,1,0:T(8,128)(2,1)S(1)}, bf16[2,64,256]{2,1,0:T(8,128)(2,1)S(1)}, u32[]{:S(2)}, u32[]{:S(2)}) collective-permute-start(bf16[2,64,256]{2,1,0:T(8,128)(2,1)S(1)} %get-tuple-element.56), channel_id=1, source_target_pairs={{1,2},{3,4},{5,6},{7,8},{9,10},{11,12},{13,14},{15,16},{17,18},{19... | collective-permute-start | bytes 196616 | tf_op jit(solution)/shard_map/ppermute | solution.py:298
  11.2 5.7 %collective-permute-start = (bf16[2,64,256]{2,1,0:T(8,128)(2,1)S(1)}, bf16[2,64,256]{2,1,0:T(8,128)(2,1)S(1)}, u32[]{:S(2)}, u32[]{:S(2)}) collective-permute-start(bf16[2,64,256]{2,1,0:T(8,128)(2,1)S(1)} %get-tuple-element.57), channel_id=1, source_target_pairs={{0,1},{2,3},{4,5},{6,7},{8,9},{10,11},{12,13},{14,15},{16,17},{18,... | collective-permute-start | bytes 196616 | tf_op jit(solution)/shard_map/ppermute | solution.py:297
  13.1 1.0 %copy-start.1 = (bf16[1,4,4,128,128]{4,3,2,1,0:T(8,128)(2,1)S(1)}, bf16[1,4,4,128,128]{4,3,2,1,0:T(8,128)(2,1)}, u32[]{:S(2)}) copy-start(bf16[1,4,4,128,128]{4,3,2,1,0:T(8,128)(2,1)} %param.6) | copy-start | bytes 1572868
  14.2 1.0 %copy-start.3 = (bf16[3,256,256]{2,1,0:T(8,128)(2,1)S(1)}, bf16[3,256,256]{2,1,0:T(8,128)(2,1)}, u32[]{:S(2)}) copy-start(bf16[3,256,256]{2,1,0:T(8,128)(2,1)} %time_ref.3) | copy-start | bytes 1179652
  14.5 2.4 %copy-start = (bf16[3,3,256,256]{3,2,1,0:T(8,128)(2,1)S(1)}, bf16[3,3,256,256]{3,2,1,0:T(8,128)(2,1)}, u32[]{:S(2)}) copy-start(bf16[3,3,256,256]{3,2,1,0:T(8,128)(2,1)} %weight_ref.3) | copy-start | bytes 3538948
  14.5 2.4 %copy-start.4 = (bf16[1,2,2,64,256]{4,3,2,1,0:T(8,128)(2,1)S(1)}, bf16[1,2,2,64,256]{4,3,2,1,0:T(8,128)(2,1)}, u32[]{:S(2)}) copy-start(bf16[1,2,2,64,256]{4,3,2,1,0:T(8,128)(2,1)} %param.5) | copy-start | bytes 393220
  19.1 4.6 %collective-permute-start.3 = (bf16[8,32,16,128]{3,2,1,0:T(8,128)(2,1)S(1)}, bf16[8,32,16,128]{3,2,1,0:T(8,128)(2,1)S(1)}, u32[]{:S(2)}, u32[]{:S(2)}) collective-permute-start(bf16[8,32,16,128]{3,2,1,0:T(8,128)(2,1)S(1)} %get-tuple-element.38), channel_id=1, source_target_pairs={{0,32},{32,0},{1,33},{33,1},{2,34},{34,2},{3,35},{35,3},{4,36},{36... | collective-permute-start | bytes 3145736 | tf_op jit(solution)/shard_map/ppermute | solution.py:318
  24.8 30.0 %all-to-all-start = ((bf16[32,8,16,128]{3,2,1,0:T(8,128)(2,1)}), bf16[32,8,16,128]{3,2,1,0:T(8,128)(2,1)S(1)}, u32[]{:S(2)}, u32[]{:S(2)}) async-start(bf16[32,8,16,128]{3,2,1,0:T(8,128)(2,1)} %bitcast.7), calls=%async_computation | async-start | bytes 2097152 | tf_op jit(solution)/shard_map/all_to_all | solution.py:322
  38.1 5.1 %collective-permute-start.5 = (bf16[2,64,256]{2,1,0:T(8,128)(2,1)S(1)}, bf16[2,64,256]{2,1,0:T(8,128)(2,1)S(1)}, u32[]{:S(2)}, u32[]{:S(2)}) collective-permute-start(bf16[2,64,256]{2,1,0:T(8,128)(2,1)S(1)} %get-tuple-element.52), channel_id=1, source_target_pairs={{1,2},{3,4},{5,6},{7,8},{9,10},{11,12},{13,14},{15,16},{17,18},{19... | collective-permute-start | bytes 196616 | tf_op jit(solution)/shard_map/ppermute | solution.py:298
  38.8 13.4 %collective-permute-start.4 = (bf16[2,64,256]{2,1,0:T(8,128)(2,1)S(1)}, bf16[2,64,256]{2,1,0:T(8,128)(2,1)S(1)}, u32[]{:S(2)}, u32[]{:S(2)}) collective-permute-start(bf16[2,64,256]{2,1,0:T(8,128)(2,1)S(1)} %get-tuple-element.53), channel_id=1, source_target_pairs={{0,1},{2,3},{4,5},{6,7},{8,9},{10,11},{12,13},{14,15},{16,17},{18,... | collective-permute-start | bytes 196616 | tf_op jit(solution)/shard_map/ppermute | solution.py:297
  55.5 17.8 %all-to-all-start.1 = ((bf16[8,16,128]{2,1,0:T(8,128)(2,1)}), bf16[8,16,128]{2,1,0:T(8,128)(2,1)S(1)}, u32[]{:S(2)}, u32[]{:S(2)}) async-start(bf16[8,16,128]{2,1,0:T(8,128)(2,1)} %shard_map.88), calls=%async_computation.1 | async-start | bytes 65536 | tf_op jit(solution)/shard_map/all_to_all | solution.py:326

commit v4 on v2

--- a/solution.py
+++ b/solution.py
@@ -9,7 +9,7 @@
 TIME = ("x", "core")
 SPACE = ("y_hi", "z_hi", "z_lo")
 GROUP = ("y_lo", "x", "core")
-NEAR = ("y_lo", "x", "y_hi", "z_lo")
+NEAR = ("z_lo", "y_hi", "y_lo", "x")
 C = 256
 W = 64
 FRAMES = 2
@@ -190,8 +190,8 @@
     for at in range(8):
         total = (mine_ref[at] + arrived_ref[at]).reshape(2, 8, 2, 16, 128)
         for low in range(2):
-            held_ref[at, :, low] = total[:, :, low]
-        copies.append(pltpu.make_async_copy(held_ref.at[at], out_ref.at[at], sems.at[at]))
+            held_ref[at, low] = total[:, :, low]
+        copies.append(pltpu.make_async_copy(held_ref.at[at], out_ref.at[:, :, at], sems.at[at]))
         copies[-1].start()
     for copy in copies:
         copy.wait()
@@ -260,14 +260,16 @@
 
 
 def swap_sum(*operands):
-    out = shape((8, 2, 2, 8, 16, 128), bf16)
+    out = shape((2, 2, 8, 8, 16, 128), bf16)
     return call(
         swap_sum_kernel,
         out,
         0,
         *operands,
         out_specs=pl.BlockSpec(memory_space=pl.ANY),
-        scratch_shapes=[pltpu.VMEM(out.shape, bf16), pltpu.SemaphoreType.DMA((8,))],
+        scratch_shapes=[
+            pltpu.VMEM((8, 2, 2, 8, 16, 128), bf16), pltpu.SemaphoreType.DMA((8,))
+        ],
     )
 
 

time: 86.4 us -> 86.3 us (level)
  waiting for transfers between devices: 14.4 us -> 13 us
  blocking collectives: 30.6 us -> 31.9 us
    all_to_all x1, waiting for transfers between devices: 1.4 us -> 0.01 us  [local(): value = lax.all_to_all(value.reshape(32, 8, 16, 128), NEAR, 0, 0)]
    all_to_all x1, blocking collectives: 12.8 us -> 13.8 us  [local(): lax.all_to_all(value, GROUP, 0, 0)]
  transfers between devices with their start and end apart: 7 -> 7, of which waited for: 4 -> 3; matrix products, arithmetic and copies ran while one was open for 1% -> 1% of each run, Pallas kernels for 2% -> 2%
where the time goes in v4:
time: 86.3 us; the launch traced here: 85.7 us
  starting transfers between devices  31.9 us (37%)
  blocking collectives  31.9 us (37%)
  waiting for transfers between devices  13 us (15%)
  Pallas kernels  6.09 us (7%)
  local copies, waits for them, and re-layouts  1.98 us (2%)
  between operations  0.87 us (1%)
    all_to_all x1, blocking collectives, local(): value = lax.all_to_all(value, 'z_hi', 0, 0)  18.1 us
    all_to_all x1, blocking collectives, local(): lax.all_to_all(value, GROUP, 0, 0)  13.8 us
    all_to_all x1, starting transfers between devices, local(): value = lax.all_to_all(value.reshape(32, 8, 16, 128), NEAR, 0, 0)  13 us
    ppermute x2, waiting for transfers between devices, halo(): first = lax.ppermute(jnp.where(even, bottom, top), SPACE, pairs[0])  10.7 us
    ppermute x1, starting transfers between devices, local(): later = lax.ppermute(cotangent, TIME, [(i + 1, i) for i in range(7)])  8.92 us
    ppermute x2, starting transfers between devices, halo(): first = lax.ppermute(jnp.where(even, bottom, top), SPACE, pairs[0])  6.32 us
    pallas_call x8, Pallas kernels, call(): pl.pallas_call(kernel, out_shape=outs, compiler_params=pltpu.CompilerPara...  6.09 us
    ppermute x1, starting transfers between devices, local(): other = lax.ppermute(other, 'core', [(0, 1), (1, 0)])  2.3 us
  transfers between devices with their start and end apart: 7, of which 3 were waited for; matrix products, arithmetic and copies ran while one was open for 1% of the time, Pallas kernels for 2%

profile of v4, /device:TPU:1, one launch (start us, length us, event | category | flops | bytes accessed | tf_op | source)
XLA Modules:
  0.0 85.7 jit_solution(10785001565847723740)
XLA Ops:
  0.6 0.0 copy-start.1
  0.6 8.9 %collective-permute-start.2 = (bf16[4,4,128,128]{3,2,1,0:T(8,128)(2,1)}, bf16[4,4,128,128]{3,2,1,0:T(8,128)(2,1)S(1)}, u32[]{:S(2)}, u32[]{:S(2)}) collective-permute-start(bf16[4,4,128,128]{3,2,1,0:T(8,128)(2,1)} %bitcast.24), channel_id=1, source_target_pairs={{32,0},{64,32},{96,64},{128,96},{160,128},{192,160},{224,192},{33,... | collective-permute-start | bytes 1572872 | tf_op jit(solution)/shard_map/ppermute | solution.py:300
  9.6 0.9 %copy.20 = bf16[1,2,2,64,256]{4,3,1,2,0:T(8,128)(2,1)S(1)} copy(bf16[1,2,2,64,256]{4,3,2,1,0:T(8,128)(2,1)} %param.5) | data formatting | bytes 262144 | tf_op args[0]
  10.5 0.7 collective-permute-start.1
  11.2 1.9 %collective-permute-start = (bf16[2,64,256]{2,1,0:T(8,128)(2,1)S(1)}, bf16[2,64,256]{2,1,0:T(8,128)(2,1)S(1)}, u32[]{:S(2)}, u32[]{:S(2)}) collective-permute-start(bf16[2,64,256]{2,1,0:T(8,128)(2,1)S(1)} %get-tuple-element.55), channel_id=1, source_target_pairs={{0,1},{2,3},{4,5},{6,7},{8,9},{10,11},{12,13},{14,15},{16,17},{18,... | collective-permute-start | bytes 196616 | tf_op jit(solution)/shard_map/ppermute | solution.py:291
  13.1 0.0 copy-start.2
  13.2 1.0 %copy-done.2 = bf16[1,4,4,128,128]{4,3,2,1,0:T(8,128)(2,1)S(1)} copy-done((bf16[1,4,4,128,128]{4,3,2,1,0:T(8,128)(2,1)S(1)}, bf16[1,4,4,128,128]{4,3,2,1,0:T(8,128)(2,1)}, u32[]{:S(2)}) %copy-start.2) | copy-done | bytes 524312
  14.2 0.3 shard_map.84.up_ref
  14.5 0.0 copy-start
  14.5 0.0 copy-start.3
  14.5 0.0 copy-start.4
  14.5 0.0 collective-permute-done.2.cot_ref
  14.5 0.0 copy-done.1
  14.5 0.6 shard_map.85
  15.1 0.0 collective-permute-done.1
  15.1 1.8 %collective-permute-done = bf16[2,64,256]{2,1,0:T(8,128)(2,1)S(1)} collective-permute-done((bf16[2,64,256]{2,1,0:T(8,128)(2,1)S(1)}, bf16[2,64,256]{2,1,0:T(8,128)(2,1)S(1)}, u32[]{:S(2)}, u32[]{:S(2)}) %collective-permute-start) | collective-permute-done | bytes 65568 | tf_op jit(solution)/shard_map/ppermute | solution.py:291
  16.9 0.0 copy-done
  16.9 0.0 copy-done.3
  16.9 0.0 copy-done.4
  16.9 2.1 %shard_map.86 = (bf16[256,256]{1,0:T(8,128)(2,1)S(1)}, bf16[8,32,16,128]{3,2,1,0:T(8,128)(2,1)S(1)}, bf16[8,32,16,128]{3,2,1,0:T(8,128)(2,1)S(1)}) custom-call(s32[1]{0:T(128)} %bitcast.core_ref, bf16[2,2,64,256]{3,2,1,0:T(8,128)(2,1)S(1)} %bitcast.26, bf16[2,64,256]{2,1,0:T(8,128)(2,1)S(1)} %get-tuple-element.53.low_ref, ...), custom_call_target="tpu_custom_call" | custom-call | flops 1275068416 | bytes 5373956 | tf_op jit(solution)/shard_map/pallas_call | solution.py:51
  19.1 2.3 %collective-permute-start.3 = (bf16[8,32,16,128]{3,2,1,0:T(8,128)(2,1)S(1)}, bf16[8,32,16,128]{3,2,1,0:T(8,128)(2,1)S(1)}, u32[]{:S(2)}, u32[]{:S(2)}) collective-permute-start(bf16[8,32,16,128]{3,2,1,0:T(8,128)(2,1)S(1)} %get-tuple-element.36), channel_id=1, source_target_pairs={{0,32},{32,0},{1,33},{33,1},{2,34},{34,2},{3,35},{35,3},{4,36},{36... | collective-permute-start | bytes 3145736 | tf_op jit(solution)/shard_map/ppermute | solution.py:309
  21.4 2.3 %collective-permute-done.3.arrived_ref = bf16[8,32,16,128]{3,2,1,0:T(8,128)(2,1)S(1)} collective-permute-done((bf16[8,32,16,128]{3,2,1,0:T(8,128)(2,1)S(1)}, bf16[8,32,16,128]{3,2,1,0:T(8,128)(2,1)S(1)}, u32[]{:S(2)}, u32[]{:S(2)}) %collective-permute-start.3) | collective-permute-done | bytes 1048608 | tf_op jit(solution)/shard_map/ppermute | solution.py:309
  23.7 1.1 %shard_map.87 = bf16[2,2,8,8,16,128]{5,4,3,2,1,0:T(8,128)(2,1)} custom-call(bf16[8,32,16,128]{3,2,1,0:T(8,128)(2,1)S(1)} %get-tuple-element.35.mine_ref, bf16[8,32,16,128]{3,2,1,0:T(8,128)(2,1)S(1)} %collective-permute-done.3.arrived_ref), custom_call_target="tpu_custom_call" | custom-call | bytes 3145728 | tf_op jit(solution)/shard_map/pallas_call | solution.py:51
  24.7 13.0 %all-to-all-start = ((bf16[32,8,16,128]{3,2,1,0:T(8,128)(2,1)}), bf16[32,8,16,128]{3,2,1,0:T(8,128)(2,1)S(1)}, u32[]{:S(2)}, u32[]{:S(2)}) async-start(bf16[32,8,16,128]{3,2,1,0:T(8,128)(2,1)} %bitcast.7), calls=%async_computation | async-start | bytes 2097152 | tf_op jit(solution)/shard_map/all_to_all | solution.py:313
  37.8 0.7 collective-permute-start.5
  38.5 4.4 %collective-permute-start.4 = (bf16[2,64,256]{2,1,0:T(8,128)(2,1)S(1)}, bf16[2,64,256]{2,1,0:T(8,128)(2,1)S(1)}, u32[]{:S(2)}, u32[]{:S(2)}) collective-permute-start(bf16[2,64,256]{2,1,0:T(8,128)(2,1)S(1)} %get-tuple-element.51), channel_id=1, source_target_pairs={{0,1},{2,3},{4,5},{6,7},{8,9},{10,11},{12,13},{14,15},{16,17},{18,... | collective-permute-start | bytes 196616 | tf_op jit(solution)/shard_map/ppermute | solution.py:291
  42.9 0.0 collective-permute-done.5
  42.9 9.0 %collective-permute-done.4 = bf16[2,64,256]{2,1,0:T(8,128)(2,1)S(1)} collective-permute-done((bf16[2,64,256]{2,1,0:T(8,128)(2,1)S(1)}, bf16[2,64,256]{2,1,0:T(8,128)(2,1)S(1)}, u32[]{:S(2)}, u32[]{:S(2)}) %collective-permute-start.4) | collective-permute-done | bytes 65568 | tf_op jit(solution)/shard_map/ppermute | solution.py:291
  51.9 1.2 %shard_map.88 = bf16[256,256]{1,0:T(8,128)(2,1)} custom-call(f32[256,256]{1,0:T(8,128)S(1)} %get-tuple-element.40.state_ref, bf16[2,2,64,256]{3,2,1,0:T(8,128)(2,1)S(1)} %bitcast.23, bf16[2,64,256]{2,1,0:T(8,128)(2,1)S(1)} %get-tuple-element.49.low_ref, bf16[2,64,256]{2,1,0:T(8,128)(2,1)S(1)} %get-tuple-element.48.high_ref, bf16[3,3,256,256]{3,2,1,0:T(8,128)(2,1)S(1)} %copy-done), custom_call_target="tpu_custom_call" | custom-call | flops 301989888 | bytes 1835008 | tf_op jit(solution)/shard_map/pallas_call | solution.py:51
  53.0 0.0 all-to-all-done.parts_ref
  53.0 0.1 shard_map.89
  53.2 18.1 %all_to_all.15.parts_ref = bf16[8,16,128]{2,1,0:T(8,128)(2,1)S(1)} all-to-all(bf16[8,16,128]{2,1,0:T(8,128)(2,1)S(1)} %shard_map.89), channel_id=1, replica_groups=mesh['y_lo'=2,'x'=4,'core'=2,'y_hi'=2,'z_hi'=8,'z_lo'=2] {'z_hi'}, dimensions={0} | all-to-all | bytes 65536 | tf_op jit(solution)/shard_map/all_to_all | solution.py:318
  71.3 13.8 %all_to_all.16.in_ref = f32[16,16,128]{2,1,0:T(8,128)S(1)} all-to-all(f32[16,16,128]{2,1,0:T(8,128)S(1)} %shard_map.90), channel_id=1, replica_groups=mesh['y_lo'=2,'x'=4,'core'=2,'y_hi'=2,'z_hi'=8,'z_lo'=2] {'y_lo','x','co..., dimensions={0} | all-to-all | bytes 262144 | tf_op jit(solution)/shard_map/all_to_all | solution.py:320
  85.1 0.7 shard_map.91
  (5 shorter events, 0.1 us)
Async XLA Ops:
  0.6 13.9 %copy-start.1 = (bf16[256,1024]{1,0:T(8,128)(2,1)S(1)}, bf16[256,1024]{1,0:T(8,128)(2,1)}, u32[]{:S(2)}) copy-start(bf16[256,1024]{1,0:T(8,128)(2,1)} %weight_ref.2) | copy-start | bytes 1572868
  0.6 13.9 %collective-permute-start.2 = (bf16[4,4,128,128]{3,2,1,0:T(8,128)(2,1)}, bf16[4,4,128,128]{3,2,1,0:T(8,128)(2,1)S(1)}, u32[]{:S(2)}, u32[]{:S(2)}) collective-permute-start(bf16[4,4,128,128]{3,2,1,0:T(8,128)(2,1)} %bitcast.24), channel_id=1, source_target_pairs={{32,0},{64,32},{96,64},{128,96},{160,128},{192,160},{224,192},{33,... | collective-permute-start | bytes 1572872 | tf_op jit(solution)/shard_map/ppermute | solution.py:300
  10.5 4.6 %collective-permute-start.1 = (bf16[2,64,256]{2,1,0:T(8,128)(2,1)S(1)}, bf16[2,64,256]{2,1,0:T(8,128)(2,1)S(1)}, u32[]{:S(2)}, u32[]{:S(2)}) collective-permute-start(bf16[2,64,256]{2,1,0:T(8,128)(2,1)S(1)} %get-tuple-element.54), channel_id=1, source_target_pairs={{1,2},{3,4},{5,6},{7,8},{9,10},{11,12},{13,14},{15,16},{17,18},{19... | collective-permute-start | bytes 196616 | tf_op jit(solution)/shard_map/ppermute | solution.py:292
  11.2 5.7 %collective-permute-start = (bf16[2,64,256]{2,1,0:T(8,128)(2,1)S(1)}, bf16[2,64,256]{2,1,0:T(8,128)(2,1)S(1)}, u32[]{:S(2)}, u32[]{:S(2)}) collective-permute-start(bf16[2,64,256]{2,1,0:T(8,128)(2,1)S(1)} %get-tuple-element.55), channel_id=1, source_target_pairs={{0,1},{2,3},{4,5},{6,7},{8,9},{10,11},{12,13},{14,15},{16,17},{18,... | collective-permute-start | bytes 196616 | tf_op jit(solution)/shard_map/ppermute | solution.py:291
  13.1 1.0 %copy-start.2 = (bf16[1,4,4,128,128]{4,3,2,1,0:T(8,128)(2,1)S(1)}, bf16[1,4,4,128,128]{4,3,2,1,0:T(8,128)(2,1)}, u32[]{:S(2)}) copy-start(bf16[1,4,4,128,128]{4,3,2,1,0:T(8,128)(2,1)} %param.6) | copy-start | bytes 1572868
  14.5 2.4 %copy-start = (bf16[3,3,256,256]{3,2,1,0:T(8,128)(2,1)S(1)}, bf16[3,3,256,256]{3,2,1,0:T(8,128)(2,1)}, u32[]{:S(2)}) copy-start(bf16[3,3,256,256]{3,2,1,0:T(8,128)(2,1)} %weight_ref.3) | copy-start | bytes 3538948
  14.5 2.4 %copy-start.3 = (bf16[1,2,2,64,256]{4,3,2,1,0:T(8,128)(2,1)S(1)}, bf16[1,2,2,64,256]{4,3,2,1,0:T(8,128)(2,1)}, u32[]{:S(2)}) copy-start(bf16[1,2,2,64,256]{4,3,2,1,0:T(8,128)(2,1)} %param.5) | copy-start | bytes 393220
  14.5 2.4 %copy-start.4 = (bf16[3,256,256]{2,1,0:T(8,128)(2,1)S(1)}, bf16[3,256,256]{2,1,0:T(8,128)(2,1)}, u32[]{:S(2)}) copy-start(bf16[3,256,256]{2,1,0:T(8,128)(2,1)} %time_ref.1) | copy-start | bytes 1179652
  19.1 4.6 %collective-permute-start.3 = (bf16[8,32,16,128]{3,2,1,0:T(8,128)(2,1)S(1)}, bf16[8,32,16,128]{3,2,1,0:T(8,128)(2,1)S(1)}, u32[]{:S(2)}, u32[]{:S(2)}) collective-permute-start(bf16[8,32,16,128]{3,2,1,0:T(8,128)(2,1)S(1)} %get-tuple-element.36), channel_id=1, source_target_pairs={{0,32},{32,0},{1,33},{33,1},{2,34},{34,2},{3,35},{35,3},{4,36},{36... | collective-permute-start | bytes 3145736 | tf_op jit(solution)/shard_map/ppermute | solution.py:309
  24.7 28.3 %all-to-all-start = ((bf16[32,8,16,128]{3,2,1,0:T(8,128)(2,1)}), bf16[32,8,16,128]{3,2,1,0:T(8,128)(2,1)S(1)}, u32[]{:S(2)}, u32[]{:S(2)}) async-start(bf16[32,8,16,128]{3,2,1,0:T(8,128)(2,1)} %bitcast.7), calls=%async_computation | async-start | bytes 2097152 | tf_op jit(solution)/shard_map/all_to_all | solution.py:313
  37.8 5.1 %collective-permute-start.5 = (bf16[2,64,256]{2,1,0:T(8,128)(2,1)S(1)}, bf16[2,64,256]{2,1,0:T(8,128)(2,1)S(1)}, u32[]{:S(2)}, u32[]{:S(2)}) collective-permute-start(bf16[2,64,256]{2,1,0:T(8,128)(2,1)S(1)} %get-tuple-element.50), channel_id=1, source_target_pairs={{1,2},{3,4},{5,6},{7,8},{9,10},{11,12},{13,14},{15,16},{17,18},{19... | collective-permute-start | bytes 196616 | tf_op jit(solution)/shard_map/ppermute | solution.py:292
  38.5 13.4 %collective-permute-start.4 = (bf16[2,64,256]{2,1,0:T(8,128)(2,1)S(1)}, bf16[2,64,256]{2,1,0:T(8,128)(2,1)S(1)}, u32[]{:S(2)}, u32[]{:S(2)}) collective-permute-start(bf16[2,64,256]{2,1,0:T(8,128)(2,1)S(1)} %get-tuple-element.51), channel_id=1, source_target_pairs={{0,1},{2,3},{4,5},{6,7},{8,9},{10,11},{12,13},{14,15},{16,17},{18,... | collective-permute-start | bytes 196616 | tf_op jit(solution)/shard_map/ppermute | solution.py:291
